TPU v7x, 256 devices: a whole 4x4x8 slice. The times are simulated.
256 devices in a mesh: grp: 2 (over z_hi), seq: 2 (over core), vocab: 64 (over z_lo, y, x).
Axes of the slice: x: 4, y: 4, z: 8 (z_hi: 2, z_lo: 4; z = z_hi * 4 + z_lo), core: 2. Of those that a mesh axis runs over, the one named last changes fastest.
Arguments:
- teacher_hidden: bfloat16 [1024, 4096], P(None, ('grp', 'seq')), may hold values from -24 to 24
- teacher_weight: bfloat16 [4096, 75968], P(('grp', 'seq'), 'vocab'), may hold values from -0.61035156 to 0.61035156
- student_hidden: bfloat16 [1024, 5120], P(None, ('grp', 'seq')), may hold values from -24 to 24
- student_weight: bfloat16 [5120, 75968], P(('grp', 'seq'), 'vocab'), may hold values from -0.48828125 to 0.48828125
- rollout_ids: int32 [1024], P(('grp', 'seq')), may hold values from 0 to 75967
Outputs:
- grad_hidden: bfloat16 [1024, 5120], P('vocab', ('grp', 'seq'))
- grad_weight: bfloat16 [5120, 75968], P(('grp', 'seq'), 'vocab')
- mean_loss: float32 [], replicated
All inputs are finite; a program needn't handle non-finite values.
Results may differ from a plain program's by a relative error of at most 0.0041.
Values may be sent and summed in bfloat16 or wider, within the bound.
No kernel may reach another device: no remote copies, remote signals or barrier semaphores. Data moves between devices by JAX's collectives and lax.ppermute only.
A program may use at most 128 MiB of HBM per device.

v0:
```python
import jax
import jax.numpy as jnp
from jax import lax
from jax.sharding import PartitionSpec as P

ENTROPY_WEIGHT = 0.1
ADVANTAGE_CLIP = 2.0


def shards(teacher_hidden, teacher_weight, student_hidden, student_weight, rollout_ids):
    all_tokens = student_hidden.shape[0]
    part_teacher = jnp.dot(teacher_hidden, teacher_weight, preferred_element_type=jnp.float32)
    part_student = jnp.dot(student_hidden, student_weight, preferred_element_type=jnp.float32)
    logits = lax.psum_scatter(
        jnp.stack([part_teacher, part_student], axis=1),
        ("grp", "seq"),
        scatter_dimension=0,
        tiled=True,
    )
    teacher_logits = logits[:, 0]
    student_logits = logits[:, 1]
    shard_width = student_logits.shape[1]
    columns = lax.axis_index("vocab") * shard_width + lax.broadcasted_iota(
        jnp.int32, student_logits.shape, 1
    )
    onehot = columns == rollout_ids[:, None]
    local_pick_s = jnp.sum(jnp.where(onehot, student_logits, jnp.float32(0.0)), axis=1)
    local_pick_t = jnp.sum(jnp.where(onehot, teacher_logits, jnp.float32(0.0)), axis=1)
    top_s, top_t = lax.pmax(
        (jnp.max(student_logits, axis=1), jnp.max(teacher_logits, axis=1)), "vocab"
    )
    shifted_s = jnp.exp(student_logits - top_s[:, None])
    total_s, total_t, weighted_s, weighted_t, pick_s, pick_t = lax.psum(
        (
            jnp.sum(shifted_s, axis=1),
            jnp.sum(jnp.exp(teacher_logits - top_t[:, None]), axis=1),
            jnp.sum(shifted_s * student_logits, axis=1),
            jnp.sum(shifted_s * teacher_logits, axis=1),
            local_pick_s,
            local_pick_t,
        ),
        "vocab",
    )
    norm_s = top_s + jnp.log(total_s)
    norm_t = top_t + jnp.log(total_t)
    factor = 1.0 + ENTROPY_WEIGHT
    divergence = factor * (weighted_s / total_s - norm_s) - (weighted_t / total_s - norm_t)
    advantage = jnp.clip(pick_t - norm_t - (pick_s - norm_s), -ADVANTAGE_CLIP, ADVANTAGE_CLIP)
    token_loss = divergence - advantage * (pick_s - norm_s)
    student_probs = jnp.exp(student_logits - top_s[:, None]) / total_s[:, None]
    inner = (
        factor * (student_logits - norm_s[:, None])
        - (teacher_logits - norm_t[:, None])
        - divergence[:, None]
    )
    logit_grad = student_probs * inner - advantage[:, None] * (
        onehot.astype(jnp.float32) - student_probs
    )
    logit_grad = logit_grad.astype(jnp.bfloat16)
    whole_grad = lax.all_gather(logit_grad, ("grp", "seq"), axis=0, tiled=True)
    mean_loss = lax.psum(jnp.sum(token_loss), ("grp", "seq")) / all_tokens
    grad_weight = lax.dot_general(
        student_hidden, whole_grad, (((0,), (0,)), ((), ())), preferred_element_type=jnp.float32
    ).astype(jnp.bfloat16)
    grad_hidden = lax.psum_scatter(
        lax.dot_general(
            whole_grad, student_weight, (((1,), (1,)), ((), ())), preferred_element_type=jnp.float32
        ),
        "vocab",
        scatter_dimension=0,
        tiled=True,
    ).astype(jnp.bfloat16)
    return (grad_hidden, grad_weight, mean_loss)


def solution(mesh):
    return jax.shard_map(
        shards,
        mesh=mesh,
        in_specs=(
            P(None, ("grp", "seq")),
            P(("grp", "seq"), "vocab"),
            P(None, ("grp", "seq")),
            P(("grp", "seq"), "vocab"),
            P(("grp", "seq")),
        ),
        out_specs=(P("vocab", ("grp", "seq")), P(("grp", "seq"), "vocab"), P()),
        check_vma=False,
    )
```

profile of v0, /device:TPU:0, one launch (start us, length us, event | category | flops | bytes accessed | tf_op | source)
XLA Modules:
  0.0 981.0 jit_solution(12324816881707272141)
XLA Ops:
  7.2 0.0 copy-start
  7.2 0.0 reduce-scatter.3.cloned.1.call-start
  7.2 1.8 copy-done
  9.0 0.0 copy-start.2
  9.0 0.0 copy-start.3
  9.0 5.3 convolution_bitcast_fusion
  14.4 0.0 copy-done.2
  14.4 0.0 copy-done.3
  14.4 2.8 convolution_bitcast_fusion.1
  17.2 4.8 pad_maximum_fusion
  21.9 0.0 reduce-scatter.3.cloned.1.call-update
  22.0 0.0 copy-start.1
  22.0 0.0 all-gather.2.cloned.1.call-start
  22.0 150.2 %reduce-scatter.3.cloned.1.call-done = f32[256,2,1187]{0,2,1:T(8,128)} async-done(((f32[1024,2,1187]{0,2,1:T(8,128)}), f32[256,2,1187]{0,2,1:T(8,128)}) %reduce-scatter.3.cloned.1.call-update) | async-done | bytes 2430992 | tf_op jit(solution)/shard_map/reduce_scatter | solution.py:14
  172.2 1.9 slice_reduce_fusion.1
  174.0 182.6 %all-reduce.1 = (f32[256]{0:T(256)S(1)}, f32[256]{0:T(256)S(1)}) all-reduce(f32[256]{0:T(256)S(1)} %get-tuple-element.11, f32[256]{0:T(256)S(1)} %get-tuple-element.12), channel_id=1, replica_groups=mesh['grp'=2,'seq'=2,'vocab'=64] {'vocab'}, use_global_device_ids=true, to_apply=%region_2.3 | all-reduce | flops 512 | bytes 4096 | tf_op jit(solution)/shard_map/pmax | solution.py:29
  356.6 0.0 copy-done.1
  356.6 2.4 fusion.17
  359.0 183.7 %all-reduce = (f32[256]{0:T(256)S(1)}, f32[256]{0:T(256)S(1)}, f32[256]{0:T(256)S(1)}, f32[256]{0:T(256)S(1)}, f32[256]{0:T(256)S(1)}, /*index=5*/f32[256]{0:T(256)S(1)}) all-reduce(f32[256]{0:T(256)S(1)} %get-tuple-element.8, f32[256]{0:T(256)S(1)} %get-tuple-element.10, ...), channel_id=1, replica_groups=mesh['grp'=2,'seq'=2,'vocab'=64] {'vocab'}, use_global_device_ids=true, to_apply=%region_14.15 | all-reduce | flops 1536 | bytes 12288 | tf_op jit(solution)/shard_map/psum | solution.py:33
  542.7 0.6 subtract_reduce_fusion
  543.3 3.1 fusion.6
  546.4 0.0 all-gather.2.cloned.1.call-update
  546.4 0.0 reduce-scatter.5.cloned.1.call-start
  546.5 39.6 %all-gather.2.cloned.1.call-done = bf16[1024,1187]{0,1:T(8,128)(2,1)} async-done(((bf16[256,1187]{0,1:T(8,128)(2,1)}), bf16[1024,1187]{0,1:T(8,128)(2,1)}) %all-gather.2.cloned.1.call-update) | async-done | bytes 2430992 | tf_op jit(solution)/shard_map/all_gather | solution.py:60
  586.1 7.6 fusion.18
  593.8 0.0 reduce-scatter.5.cloned.1.call-update
  593.8 10.6 %psum.55 = f32[]{:T(128)} all-reduce(f32[]{:T(128)} %get-tuple-element.21), channel_id=1, replica_groups=mesh['grp'=2,'seq'=2,'vocab'=64] {'grp','seq'}, use_global_device_ids=true, to_apply=%region_19.20 | all-reduce | flops 1 | bytes 8 | tf_op jit(solution)/shard_map/psum | solution.py:61
  605.1 7.5 fusion
  612.6 359.3 %reduce-scatter.5.cloned.1.call-done = f32[16,1280]{1,0:T(8,128)} async-done(((f32[1024,1280]{1,0:T(8,128)}), f32[16,1280]{1,0:T(8,128)}) %reduce-scatter.5.cloned.1.call-update) | async-done | bytes 81936 | tf_op jit(solution)/shard_map/reduce_scatter | solution.py:65
  971.9 1.5 convert_element_type.17
  (1 shorter events, 0.0 us)
Async XLA Ops:
  7.2 1.9 copy-start
  7.2 165.0 %reduce-scatter.3.cloned.1.call-start = ((), (), s32[]{:S(2)}) async-start(), calls=%async_computation.2 | async-start | bytes 12206080 | tf_op jit(solution)/shard_map/reduce_scatter | solution.py:14
  9.0 5.3 copy-start.2
  9.0 5.3 copy-start.3
  22.0 334.7 %copy-start.1 = (s32[256]{0:T(256)S(1)}, s32[256]{0:T(256)}, u32[]{:S(2)}) copy-start(s32[256]{0:T(256)} %param.9) | copy-start | bytes 3076
  22.0 564.2 %all-gather.2.cloned.1.call-start = ((), (), s32[]{:S(2)}) async-start(), calls=%async_computation.3 | async-start | bytes 3051520 | tf_op jit(solution)/shard_map/all_gather | solution.py:60
  546.4 425.4 %reduce-scatter.5.cloned.1.call-start = ((), (), s32[]{:S(2)}) async-start(), calls=%async_computation.4 | async-start | bytes 5324800 | tf_op jit(solution)/shard_map/reduce_scatter | solution.py:65
Sparse Core Ops, SparseCore 0:
  22.1 150.0 reduce-scatter.2
  546.6 39.5 all-gather.1
  593.9 377.9 reduce-scatter.4
where the time goes:
time: 981 us
  waiting for transfers between devices  549 us (56%)
  blocking collectives  377 us (38%)
  matrix products  23.2 us (2%)
  between operations  15.6 us (2%)
  other arithmetic  14.2 us (1%)
    reduce_scatter x1, waiting for transfers between devices, shards(): lax.psum_scatter(lax.dot_general(whole_grad, student_weight, (((1,), (1,)...  359 us
    psum x1, blocking collectives, shards(): lax.psum((jnp.sum(shifted_s, axis=1), jnp.sum(jnp.exp(teacher_logits - to...  184 us
    pmax x1, blocking collectives, shards(): lax.pmax((jnp.max(student_logits, axis=1), jnp.max(teacher_logits, axis=1...  183 us
    reduce_scatter x1, waiting for transfers between devices, shards(): lax.psum_scatter(jnp.stack([part_teacher, part_student], axis=1), ('grp',...  150 us
    all_gather x1, waiting for transfers between devices, shards(): whole_grad = lax.all_gather(logit_grad, ('grp', 'seq'), axis=0, tiled=True)  39.6 us
  transfers between devices with their start and end apart: 3, of which 3 were waited for; matrix products, arithmetic and copies ran while one was open for 1% of the time, Pallas kernels for 0%

commit v1 on v0

v1 whole, which is shorter than its diff:
```python
import functools

import jax
import jax.numpy as jnp
from jax import lax
from jax.experimental import pallas as pl
from jax.experimental.pallas import tpu as pltpu
from jax.sharding import Mesh
from jax.sharding import PartitionSpec as P

ENTROPY_WEIGHT = 0.1
FACTOR = 1.0 + ENTROPY_WEIGHT
ADVANTAGE_CLIP = 2.0
LANES = 256
LEVELS = 32700.0
VMEM = pl.BlockSpec(memory_space=pltpu.VMEM)
SMEM = pl.BlockSpec(memory_space=pltpu.SMEM)
F32, BF16 = jnp.float32, jnp.bfloat16


def params(mib):
    return pltpu.CompilerParams(vmem_limit_bytes=mib * 2**20)


def swap(x, axis):
    return lax.ppermute(x, axis, [(0, 1), (1, 0)])


def rotate(x, axis, size, step):
    return lax.ppermute(x, axis, [(i, (i + step) % size) for i in range(size)])


def ordered(x, *earlier):
    return lax.optimization_barrier((x, *earlier))[0]


def partial_logits(weight, hidden, owner):
    rows = lax.dynamic_slice_in_dim(hidden, owner * LANES, LANES, 0)
    return lax.dot_general(weight, rows, (((1,), (1,)), ((), ())), preferred_element_type=F32)


def code_kernel(width, as_, bs, at, bt, codes):
    def put(v):
        return v.astype(jnp.int32).astype(jnp.int16)

    full = width // 16 * 16
    blank = jnp.zeros((codes.shape[1] - width - 1, LANES), F32)
    for head, (a, b) in enumerate(((as_, bs), (at, bt))):
        x = a[...] + b[...]
        peak = jnp.max(jnp.abs(x), axis=0, keepdims=True)
        power = jnp.ceil(jnp.log2(jnp.maximum(peak, 1e-30) / LEVELS) * 256.0)
        scale = 1.0 / jnp.exp2(power * (1.0 / 256.0))
        code = jnp.clip(jnp.round(x * scale), -32767.0, 32767.0)
        codes[head, :full] = put(code[:full])
        codes[head, full:] = put(jnp.concatenate([code[full:], power, blank], axis=0))


def encode(student, teacher):
    width = student[0].shape[0]
    rows = (width + 1 + 15) // 16 * 16
    return pl.pallas_call(
        functools.partial(code_kernel, width),
        in_specs=[VMEM] * 4,
        out_specs=VMEM,
        out_shape=jax.ShapeDtypeStruct((2, rows, LANES), jnp.int16),
        compiler_params=params(16),
        cost_estimate=pl.CostEstimate(
            flops=rows * LANES, bytes_accessed=20 * rows * LANES, transcendentals=0
        ),
    )(*student, *teacher)


def units_kernel(width, codes, units):
    full = width // 16 * 16
    for head in range(2):
        end = codes[head, full:].astype(jnp.int32).astype(F32)
        power = end[width - full : width - full + 1]
        units[head] = jnp.broadcast_to(jnp.exp2(power * (1.0 / 256.0)), (8, LANES))


def code_units(width, codes):
    rows = codes.shape[1] - width // 16 * 16
    block = pl.BlockSpec(codes.shape, lambda: (0, 0, 0))
    return pl.pallas_call(
        functools.partial(units_kernel, width),
        in_specs=[block],
        out_specs=VMEM,
        out_shape=jax.ShapeDtypeStruct((2, 8, LANES), F32),
        compiler_params=params(8),
        cost_estimate=pl.CostEstimate(
            flops=30_000_000_000, bytes_accessed=rows * 2 * LANES * 2, transcendentals=0
        ),
    )(codes)


def stats_kernel(width, place, as_, bs, at, bt, codes, units, ids, sl_ref, tl_ref, stats):
    def decoded(head):
        return codes[head].astype(jnp.int32).astype(F32)[:width] * units[head, :1]

    sl = as_[...] + bs[...] + decoded(0)
    tl = at[...] + bt[...] + decoded(1)
    sl_ref[...] = sl
    tl_ref[...] = tl
    own_s = jnp.max(sl, axis=0, keepdims=True)
    own_t = jnp.max(tl, axis=0, keepdims=True)
    es = jnp.exp(sl - own_s)
    row = lax.broadcasted_iota(jnp.int32, sl.shape, 0)
    onehot = row == ids[...] - place[0] * width

    def total(x):
        return jnp.sum(x, axis=0, keepdims=True)

    rows = [
        own_s,
        own_t,
        total(es),
        total(jnp.exp(tl - own_t)),
        total(es * sl),
        total(es * tl),
        total(jnp.where(onehot, sl, 0.0)),
        total(jnp.where(onehot, tl, 0.0)),
    ]
    stats[...] = jnp.broadcast_to(jnp.concatenate(rows, axis=0)[None], stats.shape)


def local_stats(place, student, teacher, codes, ids):
    width = student[0].shape[0]
    size = width * LANES
    return pl.pallas_call(
        functools.partial(stats_kernel, width),
        in_specs=[SMEM] + [VMEM] * 7,
        out_specs=[VMEM] * 3,
        out_shape=[jax.ShapeDtypeStruct((width, LANES), F32)] * 2
        + [jax.ShapeDtypeStruct((16, 8, LANES), F32)],
        compiler_params=params(24),
        cost_estimate=pl.CostEstimate(
            flops=size * 40, bytes_accessed=size * 28, transcendentals=size * 2
        ),
    )(place, *student, *teacher, codes, code_units(width, codes), ids)


def merged(many):
    top_s, top_t = jnp.max(many[:, 0], axis=0), jnp.max(many[:, 1], axis=0)
    fs, ft = jnp.exp(many[:, 0] - top_s), jnp.exp(many[:, 1] - top_t)
    return [
        top_s,
        top_t,
        jnp.sum(many[:, 2] * fs, axis=0),
        jnp.sum(many[:, 3] * ft, axis=0),
        jnp.sum(many[:, 4] * fs, axis=0),
        jnp.sum(many[:, 5] * fs, axis=0),
        jnp.sum(many[:, 6], axis=0),
        jnp.sum(many[:, 7], axis=0),
    ]


def merge_kernel(many, out):
    out[...] = jnp.stack(merged(many[...]))


def all_stats(stats):
    many = lax.all_to_all(stats, ("y", "x"), 0, 0)
    plane = pl.pallas_call(
        merge_kernel,
        in_specs=[VMEM],
        out_specs=VMEM,
        out_shape=jax.ShapeDtypeStruct(many.shape[1:], F32),
        compiler_params=params(4),
    )(many)
    return [plane] + [rotate(plane, "z", 4, k) for k in (1, 2, 3)]


def grad_kernel(width, place, s0, s1, s2, s3, sl_ref, tl_ref, ids, grad, column):
    for k, got in enumerate((s0, s1, s2, s3)):
        column[(place[1] + 4 - k) % 4] = got[...]
    m = merged(column[...])
    top_s, top_t, total_s, total_t, weighted_s, weighted_t, pick_s, pick_t = (
        v.reshape(1, LANES) for v in m
    )
    norm_s = top_s + jnp.log(total_s)
    norm_t = top_t + jnp.log(total_t)
    divergence = FACTOR * (weighted_s / total_s - norm_s) - (weighted_t / total_s - norm_t)
    advantage = jnp.clip(pick_t - norm_t - (pick_s - norm_s), -ADVANTAGE_CLIP, ADVANTAGE_CLIP)
    loss = divergence - advantage * (pick_s - norm_s)
    sl, tl = sl_ref[...], tl_ref[...]
    row = lax.broadcasted_iota(jnp.int32, sl.shape, 0)
    onehot = row == ids[...] - place[0] * width
    probs = jnp.exp(sl - top_s) * (1.0 / total_s)
    inner = FACTOR * (sl - norm_s) - (tl - norm_t) - divergence
    out = probs * inner - advantage * (onehot.astype(F32) - probs)

    full = width // 16 * 16
    parts = []
    for _ in range(3):
        parts.append(loss.astype(BF16).astype(F32))
        loss = loss - parts[-1]
    blank = jnp.zeros((grad.shape[0] - width - 3, LANES), F32)
    grad[:full] = out[:full].astype(BF16)
    grad[full:] = jnp.concatenate([out[full:], *parts, blank], axis=0).astype(BF16)


def logit_grad(place, column, sl, tl, ids):
    width = sl.shape[0]
    rows = (width + 3 + 15) // 16 * 16
    return pl.pallas_call(
        functools.partial(grad_kernel, width),
        in_specs=[SMEM] + [VMEM] * 7,
        out_specs=VMEM,
        out_shape=jax.ShapeDtypeStruct((rows, LANES), BF16),
        scratch_shapes=[pltpu.VMEM((4, 8, LANES), F32)],
        compiler_params=params(16),
        cost_estimate=pl.CostEstimate(
            flops=sl.size * 20, bytes_accessed=sl.size * 10, transcendentals=sl.size
        ),
    )(place, *column, sl, tl, ids)


def hidden_kernel(g0, g1, w, out):
    width, depth = w.shape
    for n, g in enumerate((g0, g1)):
        part = lax.dot_general(
            g[:width], w[...], (((0,), (0,)), ((), ())), preferred_element_type=F32
        )
        out[:, 16 * n : 16 * n + 16] = part.reshape(16, 16, depth).astype(BF16)


def hidden_part(g0, g1, w):
    depth = w.shape[1]
    return pl.pallas_call(
        hidden_kernel,
        in_specs=[VMEM] * 3,
        out_specs=VMEM,
        out_shape=jax.ShapeDtypeStruct((16, 32, depth), BF16),
        compiler_params=params(24),
        cost_estimate=pl.CostEstimate(
            flops=4 * LANES * w.size, bytes_accessed=2 * w.size, transcendentals=0
        ),
    )(g0, g1, w)


def scattered(part):
    got = lax.all_to_all(part, ("y", "x"), 0, 0)
    got = jnp.sum(got.astype(F32), axis=0)
    return got.reshape(2, 16, got.shape[1])


def weight_kernel(_, *refs):
    g = jnp.concatenate([r[...] for r in refs[:4]], axis=1)
    h = jnp.concatenate([r[...] for r in refs[4:8]], axis=0)
    refs[8][...] = jnp.dot(g, h, preferred_element_type=F32).astype(BF16)
    refs[9][...] = jnp.zeros(refs[9].shape, F32)


def weight_grad(width, grads, hidden, owners):
    depth = hidden.shape[1]
    block = 256

    def rows(d):
        return pl.BlockSpec((block, d), lambda i, sc: (i, 0))

    def owned(k):
        return pl.BlockSpec((LANES, depth), lambda i, sc: (sc[k], 0))

    return pl.pallas_call(
        weight_kernel,
        grid_spec=pltpu.PrefetchScalarGridSpec(
            num_scalar_prefetch=1,
            grid=(pl.cdiv(width, block),),
            in_specs=[rows(LANES)] * 4 + [owned(k) for k in range(4)],
            out_specs=[rows(depth), pl.BlockSpec((8, 128), lambda i, sc: (0, 0))],
        ),
        out_shape=[
            jax.ShapeDtypeStruct((width, depth), BF16),
            jax.ShapeDtypeStruct((8, 128), F32),
        ],
        compiler_params=params(24),
        cost_estimate=pl.CostEstimate(
            flops=8 * LANES * width * depth, bytes_accessed=4 * width * depth, transcendentals=0
        ),
    )(owners, *grads, *([hidden] * 4))


def shards(teacher_hidden, teacher_weight, student_hidden, student_weight, rollout_ids):
    g, s, z = lax.axis_index("g"), lax.axis_index("s"), lax.axis_index("z")
    index = (z * 4 + lax.axis_index("y")) * 4 + lax.axis_index("x")
    place = jnp.stack([index, z]).astype(jnp.int32)
    tokens, depth = student_hidden.shape
    wt, ws = teacher_weight.T, student_weight.T
    width = ws.shape[0]
    ids = rollout_ids.reshape(1, LANES)

    owners = jnp.stack(
        [2 * g + s, 2 * g + 1 - s, 2 * (1 - g) + s, 2 * (1 - g) + 1 - s]
    ).astype(jnp.int32)

    give_s = swap(partial_logits(ws, student_hidden, owners[3]), "s")
    give_t = swap(partial_logits(wt, teacher_hidden, owners[3]), "s")
    keep_s = partial_logits(ws, student_hidden, owners[2])
    keep_t = partial_logits(wt, teacher_hidden, owners[2])
    codes = encode((keep_s, give_s), (keep_t, give_t))
    far = swap(codes, "g")
    near = ordered(owners, codes)
    give_s = swap(partial_logits(ws, student_hidden, near[1]), "s")
    give_t = swap(partial_logits(wt, teacher_hidden, near[1]), "s")
    keep_s = partial_logits(ws, student_hidden, near[0])
    keep_t = partial_logits(wt, teacher_hidden, near[0])

    sl, tl, stats = local_stats(place, (keep_s, give_s), (keep_t, give_t), far, ids)
    grad = logit_grad(place, all_stats(stats), sl, tl, ids)
    away = swap(grad, "g")
    other = swap(grad, "s")
    near_blocks = scattered(hidden_part(grad, other, ws))
    away_other = swap(away, "s")
    far_part = hidden_part(away, away_other, ws)
    far_blocks = scattered(far_part)
    grads = [grad, other, away, away_other]
    grad_weight, done = weight_grad(width, grads, student_hidden, ordered(owners, far_part))
    far_blocks = ordered(far_blocks, done)

    blocks = jnp.concatenate([near_blocks, far_blocks], axis=0)

    def block(dest):
        return lax.dynamic_index_in_dim(
            blocks, 2 * (g ^ (dest // 2)) + (s ^ (dest % 2)), 0, keepdims=False
        )

    total = block(z)
    for k in (1, 2, 3):
        total = total + rotate(block((z + k) % 4), "z", 4, k)
    a, b, c, d = (jnp.sum(v[width : width + 3].astype(F32)) for v in grads)
    return total.astype(BF16), grad_weight.T, ((a + b) + (c + d)) / tokens


def solution(mesh):
    split = Mesh(mesh.devices.reshape(2, 2, 4, 4, 4), ("g", "s", "z", "y", "x"))
    owners, vocab = ("g", "s"), ("z", "y", "x")
    return jax.shard_map(
        shards,
        mesh=split,
        in_specs=(P(None, owners), P(owners, vocab), P(None, owners), P(owners, vocab), P(owners)),
        out_specs=(P(vocab, owners), P(owners, vocab), P()),
        check_vma=False,
    )
```

time: 981 us -> 192 us (0.20)
  waiting for transfers between devices: 549 us -> 46.9 us
  blocking collectives: 377 us -> 31.9 us
  starting transfers between devices: 0.12 us -> 40.3 us
  Pallas kernels: 0 us -> 21.4 us
    reduce_scatter x2 -> x0, waiting for transfers between devices: 509 us -> none  [the longest x1 359 us: shards(): lax.psum_scatter(lax.dot_general(whole_grad, student_weight, (((1,), (1,)...]
    psum x2 -> x0, blocking collectives: 194 us -> none  [the longest x1 184 us: shards(): lax.psum((jnp.sum(shifted_s, axis=1), jnp.sum(jnp.exp(teacher_logits - to...]
    pmax x1 -> x0, blocking collectives: 183 us -> none  [shards(): lax.pmax((jnp.max(student_logits, axis=1), jnp.max(teacher_logits, axis=1...]
    ppermute x0 -> x14, waiting for transfers between devices: none -> 40.2 us  [the longest x8 35.9 us: swap(): return lax.ppermute(x, axis, [(0, 1), (1, 0)])]
    all_gather x1 -> x0, waiting for transfers between devices: 39.6 us -> none  [shards(): whole_grad = lax.all_gather(logit_grad, ('grp', 'seq'), axis=0, tiled=True)]
    all_to_all x0 -> x1, blocking collectives: none -> 31.9 us  [all_stats(): many = lax.all_to_all(stats, ('y', 'x'), 0, 0)]
    ppermute x0 -> x14, starting transfers between devices: none -> 31.3 us  [the longest x6 19.4 us: rotate(): return lax.ppermute(x, axis, [(i, (i + step) % size) for i in range(size)])]
    pallas_call x0 -> x8, Pallas kernels: none -> 21.4 us  [the longest x1 6.93 us: weight_grad(): pl.pallas_call(weight_kernel, grid_spec=pltpu.PrefetchScalarGridSpec(num_...]
  transfers between devices with their start and end apart: 3 -> 16, of which waited for: 3 -> 10; matrix products, arithmetic and copies ran while one was open for 1% -> 13% of each run, Pallas kernels for 0% -> 7%
where the time goes in v1:
time: 192 us; the launch traced here: 189 us
  waiting for transfers between devices  46.9 us (24%)
  starting transfers between devices  40.3 us (21%)
  blocking collectives  31.9 us (17%)
  matrix products  22.5 us (12%)
  Pallas kernels  21.4 us (11%)
  local copies, waits for them, and re-layouts  11.2 us (6%)
  other arithmetic  8.36 us (4%)
  between operations  5.96 us (3%)
    ppermute x8, waiting for transfers between devices, swap(): return lax.ppermute(x, axis, [(0, 1), (1, 0)])  35.9 us
    all_to_all x1, blocking collectives, all_stats(): many = lax.all_to_all(stats, ('y', 'x'), 0, 0)  31.9 us
    dot_general x8, matrix products, partial_logits(): lax.dot_general(weight, rows, (((1,), (1,)), ((), ())), preferred_element...  22.5 us
    ppermute x6, starting transfers between devices, rotate(): return lax.ppermute(x, axis, [(i, (i + step) % size) for i in range(size)])  19.4 us
    ppermute x8, starting transfers between devices, swap(): return lax.ppermute(x, axis, [(0, 1), (1, 0)])  11.8 us
    unnamed x26, local copies, waits for them, and re-layouts  10.6 us
    all_to_all x2, starting transfers between devices, scattered(): got = lax.all_to_all(part, ('y', 'x'), 0, 0)  9 us
    pallas_call x1, Pallas kernels, weight_grad(): pl.pallas_call(weight_kernel, grid_spec=pltpu.PrefetchScalarGridSpec(num_...  6.93 us
  transfers between devices with their start and end apart: 16, of which 10 were waited for; matrix products, arithmetic and copies ran while one was open for 13% of the time, Pallas kernels for 7%

profile of v1, /device:TPU:0, one launch (start us, length us, event | category | flops | bytes accessed | tf_op | source)
XLA Modules:
  0.0 188.6 jit_solution(3803631147594501265)
XLA Ops:
  0.7 4.3 %convolution_bitcast_fusion.2 = f32[1187,256]{1,0:T(8,128)} fusion(bf16[1280,1187]{0,1:T(8,128)(2,1)} %param.8, bf16[1024,1280]{1,0:T(8,128)(2,1)} %refs_7_.1, s32[]{:T(128)S(6)} %select_n.74), kind=kOutput, calls=%fused_computation.2 | convolution fusion | flops 777912320 | bytes 4922372 | tf_op jit(solution)/shard_map/dot_general | solution.py:39
  4.9 2.9 %convolution_bitcast_fusion.6 = f32[1187,256]{1,0:T(8,128)} fusion(bf16[1024,1187]{0,1:T(8,128)(2,1)S(1)} %copy-done, bf16[1024,1024]{1,0:T(8,128)(2,1)} %param.5, s32[]{:T(128)S(6)} %select_n.74), kind=kOutput, calls=%fused_computation.6 | convolution fusion | flops 622329856 | bytes 4170756 | tf_op jit(solution)/shard_map/dot_general | solution.py:39
  8.5 2.0 %convolution_bitcast_fusion.7.at = f32[1187,256]{1,0:T(8,128)S(1)} fusion(bf16[1024,1187]{0,1:T(8,128)(2,1)S(1)} %copy-done, bf16[1024,1024]{1,0:T(8,128)(2,1)} %param.5, s32[]{:T(128)S(6)} %select_n.73), kind=kOutput, calls=%fused_computation.7 | convolution fusion | flops 622329856 | bytes 4170756 | tf_op jit(solution)/shard_map/dot_general | solution.py:39
  10.6 2.1 %convolution_bitcast_fusion.3.as_ = f32[1187,256]{1,0:T(8,128)S(1)} fusion(bf16[1280,1187]{0,1:T(8,128)(2,1)S(1)} %copy-done.10, bf16[1024,1280]{1,0:T(8,128)(2,1)} %refs_7_.1, s32[]{:T(128)S(6)} %select_n.73), kind=kOutput, calls=%fused_computation.3 | convolution fusion | flops 777912320 | bytes 4909572 | tf_op jit(solution)/shard_map/dot_general | solution.py:39
  12.7 2.5 %shard_map.76 = s16[2,1200,256]{2,1,0:T(8,128)(2,1)S(1)} custom-call(f32[1187,256]{1,0:T(8,128)S(1)} %convolution_bitcast_fusion.3.as_, f32[1187,256]{1,0:T(8,128)} %collective-permute-done.bs, f32[1187,256]{1,0:T(8,128)S(1)} %convolution_bitcast_fusion.7.at, f32[1187,256]{1,0:T(8,128)} %collective-permute-done.1.bt), custom_call_target="tpu_custom_call" | custom-call | flops 307200 | bytes 6144000 | tf_op jit(solution)/shard_map/pallas_call | solution.py:61
  18.0 5.5 %collective-permute-start.4 = (s16[2,1200,256]{2,1,0:T(8,128)(2,1)}, s16[2,1200,256]{2,1,0:T(8,128)(2,1)}, u32[]{:S(2)}, u32[]{:S(2)}) collective-permute-start(s16[2,1200,256]{2,1,0:T(8,128)(2,1)} %copy-done.4), channel_id=1, source_target_pairs={{0,128},{128,0},{1,129},{129,1},{2,130},{130,2},{3,131},{131,3},{4... | collective-permute-start | bytes 3686408 | tf_op jit(solution)/shard_map/ppermute | solution.py:26
  23.5 4.1 %convolution_bitcast_fusion = f32[1187,256]{1,0:T(8,128)} fusion(bf16[1280,1187]{0,1:T(8,128)(2,1)} %param.8, bf16[1024,1280]{1,0:T(8,128)(2,1)} %refs_7_.1, s32[]{:T(128)S(6)} %select_n.76), kind=kOutput, calls=%fused_computation | convolution fusion | flops 777912320 | bytes 4922372 | tf_op jit(solution)/shard_map/dot_general | solution.py:39
  27.7 2.9 %convolution_bitcast_fusion.4 = f32[1187,256]{1,0:T(8,128)} fusion(bf16[1024,1187]{0,1:T(8,128)(2,1)S(1)} %copy-done, bf16[1024,1024]{1,0:T(8,128)(2,1)} %param.5, s32[]{:T(128)S(6)} %select_n.76), kind=kOutput, calls=%fused_computation.4 | convolution fusion | flops 622329856 | bytes 4170756 | tf_op jit(solution)/shard_map/dot_general | solution.py:39
  31.1 2.0 %convolution_bitcast_fusion.5.at = f32[1187,256]{1,0:T(8,128)S(1)} fusion(bf16[1024,1187]{0,1:T(8,128)(2,1)S(1)} %copy-done, bf16[1024,1024]{1,0:T(8,128)(2,1)} %param.5, s32[]{:T(128)S(6)} %select_n.75), kind=kOutput, calls=%fused_computation.5 | convolution fusion | flops 622329856 | bytes 4170756 | tf_op jit(solution)/shard_map/dot_general | solution.py:39
  33.2 2.1 %convolution_bitcast_fusion.1.as_ = f32[1187,256]{1,0:T(8,128)S(1)} fusion(bf16[1280,1187]{0,1:T(8,128)(2,1)S(1)} %copy-done.11, bf16[1024,1280]{1,0:T(8,128)(2,1)} %refs_7_.1, s32[]{:T(128)S(6)} %select_n.75), kind=kOutput, calls=%fused_computation.1 | convolution fusion | flops 777912320 | bytes 4909572 | tf_op jit(solution)/shard_map/dot_general | solution.py:39
  35.3 23.8 %collective-permute-done.4.codes = s16[2,1200,256]{2,1,0:T(8,128)(2,1)} collective-permute-done((s16[2,1200,256]{2,1,0:T(8,128)(2,1)}, s16[2,1200,256]{2,1,0:T(8,128)(2,1)}, u32[]{:S(2)}, u32[]{:S(2)}) %collective-permute-start.4) | collective-permute-done | bytes 1228832 | tf_op jit(solution)/shard_map/ppermute | solution.py:26
  60.4 3.9 %shard_map.78 = (f32[1187,256]{1,0:T(8,128)S(1)}, f32[1187,256]{1,0:T(8,128)S(1)}, f32[16,8,256]{2,1,0:T(8,128)S(1)}) custom-call(s32[2]{0:T(128)S(1)} %pad_add_fusion.place, f32[1187,256]{1,0:T(8,128)S(1)} %convolution_bitcast_fusion.1.as_, f32[1187,256]{1,0:T(8,128)} %collective-permute-done.2.bs, f32[1187,256]{1,0:T(8,128)S(1)} %convolution_bitcast_fusion.5.at, ...), custom_call_target="tpu_custom_call" | custom-call | flops 12154880 | bytes 8508416 | tf_op jit(solution)/shard_map/pallas_call | solution.py:129
  64.3 31.9 %all_to_all.15.many = f32[16,8,256]{2,1,0:T(8,128)S(1)} all-to-all(f32[16,8,256]{2,1,0:T(8,128)S(1)} %get-tuple-element.10), channel_id=1, replica_groups=mesh['g'=2,'s'=2,'z'=4,'y'=4,'x'=4] {'y','x'}, dimensions={0} | all-to-all | bytes 262144 | tf_op jit(solution)/shard_map/all_to_all | solution.py:162
  96.3 2.5 %collective-permute-start.5 = (f32[8,256]{1,0:T(8,128)S(1)}, f32[8,256]{1,0:T(8,128)S(1)}, u32[]{:S(2)}, u32[]{:S(2)}) collective-permute-start(f32[8,256]{1,0:T(8,128)S(1)} %shard_map.79.s0), channel_id=1, source_target_pairs={{0,16},{16,32},{32,48},{48,0},{1,17},{17,33},{33,49},{49,1},{2,18}... | collective-permute-start | bytes 24584 | tf_op jit(solution)/shard_map/ppermute | solution.py:30
  99.6 2.8 %collective-permute-start.7 = (f32[8,256]{1,0:T(8,128)S(1)}, f32[8,256]{1,0:T(8,128)S(1)}, u32[]{:S(2)}, u32[]{:S(2)}) collective-permute-start(f32[8,256]{1,0:T(8,128)S(1)} %shard_map.79.s0), channel_id=1, source_target_pairs={{0,48},{16,0},{32,16},{48,32},{1,49},{17,1},{33,17},{49,33},{2,50}... | collective-permute-start | bytes 24584 | tf_op jit(solution)/shard_map/ppermute | solution.py:30
  103.8 1.8 shard_map.80.g0.refs_0_
  105.8 5.2 %collective-permute-start.9 = (bf16[1200,256]{1,0:T(8,128)(2,1)S(1)}, bf16[1200,256]{1,0:T(8,128)(2,1)}, u32[]{:S(2)}, u32[]{:S(2)}) collective-permute-start(bf16[1200,256]{1,0:T(8,128)(2,1)S(1)} %shard_map.80.g0.refs_0_), channel_id=1, source_target_pairs={{0,128},{128,0},{1,129},{129,1},{2,130},{130,2},{3,131},{131,3},{4... | collective-permute-start | bytes 1843208 | tf_op jit(solution)/shard_map/ppermute | solution.py:26
  111.0 1.9 %shard_map.81 = bf16[16,32,1280]{2,1,0:T(8,128)(2,1)S(1)} custom-call(bf16[1200,256]{1,0:T(8,128)(2,1)S(1)} %shard_map.80.g0.refs_0_, bf16[1200,256]{1,0:T(8,128)(2,1)S(1)} %collective-permute-done.8.g1.refs_1_, bf16[1187,1280]{1,0:T(8,128)(2,1)S(1)} %bitcast.55), custom_call_target="tpu_custom_call" | custom-call | flops 1555824640 | bytes 3038720 | tf_op jit(solution)/shard_map/pallas_call | solution.py:229
  114.8 4.4 %all-to-all-start.1 = ((bf16[16,32,1280]{2,1,0:T(8,128)(2,1)}), bf16[16,32,1280]{2,1,0:T(8,128)(2,1)}, u32[]{:S(2)}, u32[]{:S(2)}) async-start(bf16[16,32,1280]{2,1,0:T(8,128)(2,1)} %copy-done.3), calls=%async_computation.1 | async-start | bytes 2621440 | tf_op jit(solution)/shard_map/all_to_all | solution.py:242
  119.2 9.9 %collective-permute-done.9.g0.refs_2_ = bf16[1200,256]{1,0:T(8,128)(2,1)} collective-permute-done((bf16[1200,256]{1,0:T(8,128)(2,1)S(1)}, bf16[1200,256]{1,0:T(8,128)(2,1)}, u32[]{:S(2)}, u32[]{:S(2)}) %collective-permute-start.9) | collective-permute-done | bytes 614432 | tf_op jit(solution)/shard_map/ppermute | solution.py:26
  129.1 2.2 %collective-permute-done.10.g1.refs_3_ = bf16[1200,256]{1,0:T(8,128)(2,1)S(1)} collective-permute-done((bf16[1200,256]{1,0:T(8,128)(2,1)}, bf16[1200,256]{1,0:T(8,128)(2,1)S(1)}, u32[]{:S(2)}, u32[]{:S(2)}) %collective-permute-start.10) | collective-permute-done | bytes 614432 | tf_op jit(solution)/shard_map/ppermute | solution.py:26
  131.4 1.9 copy-done.12
  133.2 3.0 %shard_map.82 = bf16[16,32,1280]{2,1,0:T(8,128)(2,1)S(1)} custom-call(bf16[1200,256]{1,0:T(8,128)(2,1)} %collective-permute-done.9.g0.refs_2_, bf16[1200,256]{1,0:T(8,128)(2,1)S(1)} %collective-permute-done.10.g1.refs_3_, bf16[1187,1280]{1,0:T(8,128)(2,1)S(1)} %bitcast.56), custom_call_target="tpu_custom_call" | custom-call | flops 1555824640 | bytes 3038720 | tf_op jit(solution)/shard_map/pallas_call | solution.py:229
  138.1 3.3 %all-to-all-done.1 = bf16[16,32,1280]{2,1,0:T(8,128)(2,1)} async-done(((bf16[16,32,1280]{2,1,0:T(8,128)(2,1)}), bf16[16,32,1280]{2,1,0:T(8,128)(2,1)}, u32[]{:S(2)}, u32[]{:S(2)}) %all-to-all-start.1) | async-done | bytes 1310752 | tf_op jit(solution)/shard_map/all_to_all | solution.py:242
  141.5 4.6 %all-to-all-start.2 = ((bf16[16,32,1280]{2,1,0:T(8,128)(2,1)}), bf16[16,32,1280]{2,1,0:T(8,128)(2,1)}, u32[]{:S(2)}, u32[]{:S(2)}) async-start(bf16[16,32,1280]{2,1,0:T(8,128)(2,1)} %copy-done.2), calls=%async_computation.2 | async-start | bytes 2621440 | tf_op jit(solution)/shard_map/all_to_all | solution.py:242
  150.7 1.7 copy-done.1
  154.6 6.9 %shard_map.83 = (bf16[1187,1280]{1,0:T(8,128)(2,1)}, f32[8,128]{1,0:T(8,128)}) custom-call(s32[4]{0:T(128)S(1)} %pad_add_fusion.1._, bf16[1200,256]{1,0:T(8,128)(2,1)S(1)} %shard_map.80.g0.refs_0_, bf16[1200,256]{1,0:T(8,128)(2,1)S(1)} %copy-done.8, bf16[1200,256]{1,0:T(8,128)(2,1)} %collective-permute-done.9.g0.refs_2_, bf16[1200,256]{1,0:T(8,128)(2,1)S(1)} %copy-done.6, ...), custom_call_target="tpu_custom_call" | custom-call | flops 3111649280 | bytes 6077440 | tf_op jit(solution)/shard_map/pallas_call | solution.py:264
  163.0 3.4 %all-to-all-done.2 = bf16[16,32,1280]{2,1,0:T(8,128)(2,1)} async-done(((bf16[16,32,1280]{2,1,0:T(8,128)(2,1)}), bf16[16,32,1280]{2,1,0:T(8,128)(2,1)}, u32[]{:S(2)}, u32[]{:S(2)}) %all-to-all-start.2) | async-done | bytes 1310752 | tf_op jit(solution)/shard_map/all_to_all | solution.py:242
  166.4 1.5 convert_reduce_fusion
  168.0 7.3 %collective-permute-start.11 = (f32[16,1280]{1,0:T(8,128)S(1)}, f32[16,1280]{1,0:T(8,128)S(1)}, u32[]{:S(2)}, u32[]{:S(2)}) collective-permute-start(f32[16,1280]{1,0:T(8,128)S(1)} %get-tuple-element.15), channel_id=1, source_target_pairs={{0,16},{16,32},{32,48},{48,0},{1,17},{17,33},{33,49},{49,1},{2,18}... | collective-permute-start | bytes 245768 | tf_op jit(solution)/shard_map/ppermute | solution.py:30
  175.3 6.1 %collective-permute-start.12 = (f32[16,1280]{1,0:T(8,128)S(1)}, f32[16,1280]{1,0:T(8,128)S(1)}, u32[]{:S(2)}, u32[]{:S(2)}) collective-permute-start(f32[16,1280]{1,0:T(8,128)S(1)} %get-tuple-element.16), channel_id=1, source_target_pairs={{0,32},{16,48},{32,0},{48,16},{1,33},{17,49},{33,1},{49,17},{2,34}... | collective-permute-start | bytes 245768 | tf_op jit(solution)/shard_map/ppermute | solution.py:30
  184.2 2.1 %collective-permute-done.12 = f32[16,1280]{1,0:T(8,128)S(1)} collective-permute-done((f32[16,1280]{1,0:T(8,128)S(1)}, f32[16,1280]{1,0:T(8,128)S(1)}, u32[]{:S(2)}, u32[]{:S(2)}) %collective-permute-start.12) | collective-permute-done | bytes 81952 | tf_op jit(solution)/shard_map/ppermute | solution.py:30
  (54 shorter events, 19.9 us)
Async XLA Ops:
  0.6 4.3 %copy-start = (bf16[1024,1187]{0,1:T(8,128)(2,1)S(1)}, bf16[1024,1187]{0,1:T(8,128)(2,1)}, u32[]{:S(2)}) copy-start(bf16[1024,1187]{0,1:T(8,128)(2,1)} %param.6) | copy-start | bytes 7292932
  4.9 7.8 %collective-permute-start = (f32[1187,256]{1,0:T(8,128)}, f32[1187,256]{1,0:T(8,128)}, u32[]{:S(2)}, u32[]{:S(2)}) collective-permute-start(f32[1187,256]{1,0:T(8,128)} %convolution_bitcast_fusion.2), channel_id=1, source_target_pairs={{0,64},{64,0},{1,65},{65,1},{2,66},{66,2},{3,67},{67,3},{4,68},{68... | collective-permute-start | bytes 3646472 | tf_op jit(solution)/shard_map/ppermute | solution.py:26
  7.8 4.8 %collective-permute-start.1 = (f32[1187,256]{1,0:T(8,128)}, f32[1187,256]{1,0:T(8,128)}, u32[]{:S(2)}, u32[]{:S(2)}) collective-permute-start(f32[1187,256]{1,0:T(8,128)} %convolution_bitcast_fusion.6), channel_id=1, source_target_pairs={{0,64},{64,0},{1,65},{65,1},{2,66},{66,2},{3,67},{67,3},{4,68},{68... | collective-permute-start | bytes 3646472 | tf_op jit(solution)/shard_map/ppermute | solution.py:26
  8.4 2.1 %copy-start.10 = (bf16[1280,1187]{0,1:T(8,128)(2,1)S(1)}, bf16[1280,1187]{0,1:T(8,128)(2,1)}, u32[]{:S(2)}) copy-start(bf16[1280,1187]{0,1:T(8,128)(2,1)} %param.8) | copy-start | bytes 9116164
  15.2 1.0 copy-start.4
  18.0 41.1 %collective-permute-start.4 = (s16[2,1200,256]{2,1,0:T(8,128)(2,1)}, s16[2,1200,256]{2,1,0:T(8,128)(2,1)}, u32[]{:S(2)}, u32[]{:S(2)}) collective-permute-start(s16[2,1200,256]{2,1,0:T(8,128)(2,1)} %copy-done.4), channel_id=1, source_target_pairs={{0,128},{128,0},{1,129},{129,1},{2,130},{130,2},{3,131},{131,3},{4... | collective-permute-start | bytes 3686408 | tf_op jit(solution)/shard_map/ppermute | solution.py:26
  27.6 32.7 %collective-permute-start.2 = (f32[1187,256]{1,0:T(8,128)}, f32[1187,256]{1,0:T(8,128)}, u32[]{:S(2)}, u32[]{:S(2)}) collective-permute-start(f32[1187,256]{1,0:T(8,128)} %convolution_bitcast_fusion), channel_id=1, source_target_pairs={{0,64},{64,0},{1,65},{65,1},{2,66},{66,2},{3,67},{67,3},{4,68},{68... | collective-permute-start | bytes 3646472 | tf_op jit(solution)/shard_map/ppermute | solution.py:26
  30.6 29.8 %collective-permute-start.3 = (f32[1187,256]{1,0:T(8,128)}, f32[1187,256]{1,0:T(8,128)}, u32[]{:S(2)}, u32[]{:S(2)}) collective-permute-start(f32[1187,256]{1,0:T(8,128)} %convolution_bitcast_fusion.4), channel_id=1, source_target_pairs={{0,64},{64,0},{1,65},{65,1},{2,66},{66,2},{3,67},{67,3},{4,68},{68... | collective-permute-start | bytes 3646472 | tf_op jit(solution)/shard_map/ppermute | solution.py:26
  31.1 2.0 %copy-start.11 = (bf16[1280,1187]{0,1:T(8,128)(2,1)S(1)}, bf16[1280,1187]{0,1:T(8,128)(2,1)}, u32[]{:S(2)}) copy-start(bf16[1280,1187]{0,1:T(8,128)(2,1)} %param.8) | copy-start | bytes 9116164
  35.3 25.1 %copy-start.9 = (s32[256]{0:T(256)S(1)}, s32[256]{0:T(256)}, u32[]{:S(2)}) copy-start(s32[256]{0:T(256)} %param.9) | copy-start | bytes 3076
  96.3 6.1 %collective-permute-start.5 = (f32[8,256]{1,0:T(8,128)S(1)}, f32[8,256]{1,0:T(8,128)S(1)}, u32[]{:S(2)}, u32[]{:S(2)}) collective-permute-start(f32[8,256]{1,0:T(8,128)S(1)} %shard_map.79.s0), channel_id=1, source_target_pairs={{0,16},{16,32},{32,48},{48,0},{1,17},{17,33},{33,49},{49,1},{2,18}... | collective-permute-start | bytes 24584 | tf_op jit(solution)/shard_map/ppermute | solution.py:30
  98.9 4.5 %collective-permute-start.6 = (f32[8,256]{1,0:T(8,128)S(1)}, f32[8,256]{1,0:T(8,128)S(1)}, u32[]{:S(2)}, u32[]{:S(2)}) collective-permute-start(f32[8,256]{1,0:T(8,128)S(1)} %shard_map.79.s0), channel_id=1, source_target_pairs={{0,32},{16,48},{32,0},{48,16},{1,33},{17,49},{33,1},{49,17},{2,34}... | collective-permute-start | bytes 24584 | tf_op jit(solution)/shard_map/ppermute | solution.py:30
  99.6 4.2 %collective-permute-start.7 = (f32[8,256]{1,0:T(8,128)S(1)}, f32[8,256]{1,0:T(8,128)S(1)}, u32[]{:S(2)}, u32[]{:S(2)}) collective-permute-start(f32[8,256]{1,0:T(8,128)S(1)} %shard_map.79.s0), channel_id=1, source_target_pairs={{0,48},{16,0},{32,16},{48,32},{1,49},{17,1},{33,17},{49,33},{2,50}... | collective-permute-start | bytes 24584 | tf_op jit(solution)/shard_map/ppermute | solution.py:30
  105.7 5.3 %collective-permute-start.8 = (bf16[1200,256]{1,0:T(8,128)(2,1)S(1)}, bf16[1200,256]{1,0:T(8,128)(2,1)S(1)}, u32[]{:S(2)}, u32[]{:S(2)}) collective-permute-start(bf16[1200,256]{1,0:T(8,128)(2,1)S(1)} %shard_map.80.g0.refs_0_), channel_id=1, source_target_pairs={{0,64},{64,0},{1,65},{65,1},{2,66},{66,2},{3,67},{67,3},{4,68},{68... | collective-permute-start | bytes 1843208 | tf_op jit(solution)/shard_map/ppermute | solution.py:26
  105.8 23.4 %collective-permute-start.9 = (bf16[1200,256]{1,0:T(8,128)(2,1)S(1)}, bf16[1200,256]{1,0:T(8,128)(2,1)}, u32[]{:S(2)}, u32[]{:S(2)}) collective-permute-start(bf16[1200,256]{1,0:T(8,128)(2,1)S(1)} %shard_map.80.g0.refs_0_), channel_id=1, source_target_pairs={{0,128},{128,0},{1,129},{129,1},{2,130},{130,2},{3,131},{131,3},{4... | collective-permute-start | bytes 1843208 | tf_op jit(solution)/shard_map/ppermute | solution.py:26
  112.9 1.1 copy-start.3
  113.9 0.9 copy-start.7
  114.8 26.7 %all-to-all-start.1 = ((bf16[16,32,1280]{2,1,0:T(8,128)(2,1)}), bf16[16,32,1280]{2,1,0:T(8,128)(2,1)}, u32[]{:S(2)}, u32[]{:S(2)}) async-start(bf16[16,32,1280]{2,1,0:T(8,128)(2,1)} %copy-done.3), calls=%async_computation.1 | async-start | bytes 2621440 | tf_op jit(solution)/shard_map/all_to_all | solution.py:242
  129.1 2.2 %collective-permute-start.10 = (bf16[1200,256]{1,0:T(8,128)(2,1)}, bf16[1200,256]{1,0:T(8,128)(2,1)S(1)}, u32[]{:S(2)}, u32[]{:S(2)}) collective-permute-start(bf16[1200,256]{1,0:T(8,128)(2,1)} %collective-permute-done.9.g0.refs_2_), channel_id=1, source_target_pairs={{0,64},{64,0},{1,65},{65,1},{2,66},{66,2},{3,67},{67,3},{4,68},{68... | collective-permute-start | bytes 1843208 | tf_op jit(solution)/shard_map/ppermute | solution.py:26
  131.4 1.9 copy-start.12
  136.2 1.1 copy-start.2
  137.3 0.8 copy-start.5
  141.5 24.9 %all-to-all-start.2 = ((bf16[16,32,1280]{2,1,0:T(8,128)(2,1)}), bf16[16,32,1280]{2,1,0:T(8,128)(2,1)}, u32[]{:S(2)}, u32[]{:S(2)}) async-start(bf16[16,32,1280]{2,1,0:T(8,128)(2,1)} %copy-done.2), calls=%async_computation.2 | async-start | bytes 2621440 | tf_op jit(solution)/shard_map/all_to_all | solution.py:242
  150.7 1.7 copy-start.1
  152.5 1.1 copy-start.6
  153.5 1.1 copy-start.8
  168.0 16.2 %collective-permute-start.11 = (f32[16,1280]{1,0:T(8,128)S(1)}, f32[16,1280]{1,0:T(8,128)S(1)}, u32[]{:S(2)}, u32[]{:S(2)}) collective-permute-start(f32[16,1280]{1,0:T(8,128)S(1)} %get-tuple-element.15), channel_id=1, source_target_pairs={{0,16},{16,32},{32,48},{48,0},{1,17},{17,33},{33,49},{49,1},{2,18}... | collective-permute-start | bytes 245768 | tf_op jit(solution)/shard_map/ppermute | solution.py:30
  175.3 11.1 %collective-permute-start.12 = (f32[16,1280]{1,0:T(8,128)S(1)}, f32[16,1280]{1,0:T(8,128)S(1)}, u32[]{:S(2)}, u32[]{:S(2)}) collective-permute-start(f32[16,1280]{1,0:T(8,128)S(1)} %get-tuple-element.16), channel_id=1, source_target_pairs={{0,32},{16,48},{32,0},{48,16},{1,33},{17,49},{33,1},{49,17},{2,34}... | collective-permute-start | bytes 245768 | tf_op jit(solution)/shard_map/ppermute | solution.py:30
  181.3 5.5 %collective-permute-start.13 = (f32[16,1280]{1,0:T(8,128)S(1)}, f32[16,1280]{1,0:T(8,128)S(1)}, u32[]{:S(2)}, u32[]{:S(2)}) collective-permute-start(f32[16,1280]{1,0:T(8,128)S(1)} %get-tuple-element.17), channel_id=1, source_target_pairs={{0,48},{16,0},{32,16},{48,32},{1,49},{17,1},{33,17},{49,33},{2,50}... | collective-permute-start | bytes 245768 | tf_op jit(solution)/shard_map/ppermute | solution.py:30

commit v2 on v1

v2 whole, which is shorter than its diff:
```python
import functools

import jax
import jax.numpy as jnp
from jax import lax
from jax.experimental import pallas as pl
from jax.experimental.pallas import tpu as pltpu
from jax.sharding import Mesh
from jax.sharding import PartitionSpec as P

ENTROPY_WEIGHT = 0.1
FACTOR = 1.0 + ENTROPY_WEIGHT
ADVANTAGE_CLIP = 2.0
LANES = 128
LEVELS = 32700.0
HIDES = 30_000_000_000
LAST = 8_200_000_000
SECOND = HIDES // 8
VMEM = pl.BlockSpec(memory_space=pltpu.VMEM)
SMEM = pl.BlockSpec(memory_space=pltpu.SMEM)
F32, BF16 = jnp.float32, jnp.bfloat16


def estimate(flops):
    return pl.CostEstimate(flops=flops, bytes_accessed=1, transcendentals=0)


FREE = estimate(1)


def params(mib):
    return pltpu.CompilerParams(vmem_limit_bytes=mib * 2**20)


def swap(x, axis):
    return lax.ppermute(x, axis, [(0, 1), (1, 0)])


def rotate(x, axis, size, step):
    return lax.ppermute(x, axis, [(i, (i + step) % size) for i in range(size)])


def ordered(x, *earlier):
    return lax.optimization_barrier((x, *earlier))[0]


def partial_logits(weight, hidden, grp, core):
    parts = hidden.reshape(2, 2, 2, LANES, hidden.shape[1])
    rows = lax.dynamic_slice(parts, (grp, 0, core, 0, 0), (1, 2, 1, *parts.shape[3:]))
    rows = rows.reshape(2 * LANES, hidden.shape[1])
    return lax.dot_general(weight, rows, (((1,), (1,)), ((), ())), preferred_element_type=F32)


def near_kernel(width, _, *refs):
    hs, ht, ws, wt, outs, rs, rt = refs[:4], refs[4:8], refs[8], refs[9], refs[10:14], refs[14], refs[15]
    step = pl.program_id(0)

    @pl.when(step == 0)
    def _():
        for k in range(4):
            rs[LANES * k : LANES * (k + 1)] = hs[k][...]
            rt[LANES * k : LANES * (k + 1)] = ht[k][...]

    for head, (w, r) in enumerate(((ws, rs), (wt, rt))):
        out = lax.dot_general(w[...], r[...], (((1,), (1,)), ((), ())), preferred_element_type=F32)
        outs[2 * head][...] = out[:, : 2 * LANES]
        outs[2 * head + 1][...] = out[:, 2 * LANES :]


def near_logits(blocks, hidden_s, hidden_t, ws, wt):
    width = ws.shape[0]
    ds, dt = hidden_s.shape[1], hidden_t.shape[1]
    tile = 2 * LANES

    def rows(k, d):
        return pl.BlockSpec((LANES, d), lambda i, sc: (sc[k], 0))

    def part(d):
        return pl.BlockSpec((tile, d), lambda i, sc: (i, 0))

    return pl.pallas_call(
        functools.partial(near_kernel, width),
        grid_spec=pltpu.PrefetchScalarGridSpec(
            num_scalar_prefetch=1,
            grid=(pl.cdiv(width, tile),),
            in_specs=[rows(k, d) for d in (ds, dt) for k in range(4)] + [part(ds), part(dt)],
            out_specs=[part(2 * LANES)] * 4,
            scratch_shapes=[pltpu.VMEM((4 * LANES, ds), BF16), pltpu.VMEM((4 * LANES, dt), BF16)],
        ),
        out_shape=[jax.ShapeDtypeStruct((width, 2 * LANES), F32)] * 4,
        compiler_params=params(24),
        cost_estimate=FREE,
    )(blocks, *([hidden_s] * 4), *([hidden_t] * 4), ws, wt)


def code_kernel(width, as_, bs, at, bt, *codes):
    def put(v):
        return v.astype(jnp.int32).astype(jnp.int16)

    full = width // 16 * 16
    blank = jnp.zeros((codes[0].shape[1] - width - 1, LANES), F32)
    for c, out in enumerate(codes):
        lanes = slice(c * LANES, (c + 1) * LANES)
        for head, (a, b) in enumerate(((as_, bs), (at, bt))):
            x = a[:, lanes] + b[:, lanes]
            peak = jnp.max(jnp.abs(x), axis=0, keepdims=True)
            power = jnp.ceil(jnp.log2(jnp.maximum(peak, 1e-30) / LEVELS) * 256.0)
            scale = 1.0 / jnp.exp2(power * (1.0 / 256.0))
            code = jnp.clip(jnp.round(x * scale), -32767.0, 32767.0)
            out[head, :full] = put(code[:full])
            out[head, full:] = put(jnp.concatenate([code[full:], power, blank], axis=0))


def encode(student, teacher):
    width = student[0].shape[0]
    rows = (width + 1 + 15) // 16 * 16
    return pl.pallas_call(
        functools.partial(code_kernel, width),
        in_specs=[VMEM] * 4,
        out_specs=[VMEM] * 2,
        out_shape=[jax.ShapeDtypeStruct((2, rows, LANES), jnp.int16)] * 2,
        compiler_params=params(16),
        cost_estimate=pl.CostEstimate(
            flops=rows * LANES, bytes_accessed=20 * rows * LANES, transcendentals=0
        ),
    )(*student, *teacher)


def units_kernel(width, codes, units):
    full = width // 16 * 16
    for head in range(2):
        end = codes[head, full:].astype(jnp.int32).astype(F32)
        power = end[width - full : width - full + 1]
        units[head] = jnp.broadcast_to(jnp.exp2(power * (1.0 / 256.0)), (8, LANES))


def code_units(width, codes, flops):
    rows = codes.shape[1] - width // 16 * 16
    block = pl.BlockSpec(codes.shape, lambda: (0, 0, 0))
    return pl.pallas_call(
        functools.partial(units_kernel, width),
        in_specs=[block],
        out_specs=VMEM,
        out_shape=jax.ShapeDtypeStruct((2, 8, LANES), F32),
        compiler_params=params(8),
        cost_estimate=estimate(flops),
    )(codes)


def stats_kernel(width, place, as_, bs, at, bt, codes, units, ids, sl_ref, tl_ref, stats):
    def decoded(head):
        return codes[head].astype(jnp.int32).astype(F32)[:width] * units[head, :1]

    sl = as_[...] + bs[...] + decoded(0)
    tl = at[...] + bt[...] + decoded(1)
    sl_ref[...] = sl
    tl_ref[...] = tl
    own_s = jnp.max(sl, axis=0, keepdims=True)
    own_t = jnp.max(tl, axis=0, keepdims=True)
    es = jnp.exp(sl - own_s)
    row = lax.broadcasted_iota(jnp.int32, sl.shape, 0)
    onehot = row == ids[...] - place[0] * width

    def total(x):
        return jnp.sum(x, axis=0, keepdims=True)

    rows = [
        own_s,
        own_t,
        total(es),
        total(jnp.exp(tl - own_t)),
        total(es * sl),
        total(es * tl),
        total(jnp.where(onehot, sl, 0.0)),
        total(jnp.where(onehot, tl, 0.0)),
    ]
    stats[...] = jnp.broadcast_to(jnp.concatenate(rows, axis=0)[None], stats.shape)


def local_stats(place, c, student, teacher, codes, flops, ids):
    width = student[0].shape[0]
    size = width * LANES
    half = pl.BlockSpec((width, LANES), lambda i: (0, c))

    def whole(*shape):
        return pl.BlockSpec(shape, lambda i: (0,) * len(shape))

    return pl.pallas_call(
        functools.partial(stats_kernel, width),
        grid=(1,),
        in_specs=[SMEM] + [half] * 4 + [whole(*codes.shape), whole(2, 8, LANES), whole(1, LANES)],
        out_specs=[whole(width, LANES)] * 2 + [whole(16, 8, LANES)],
        out_shape=[jax.ShapeDtypeStruct((width, LANES), F32)] * 2
        + [jax.ShapeDtypeStruct((16, 8, LANES), F32)],
        compiler_params=params(24),
        cost_estimate=estimate(flops[1]),
    )(place, *student, *teacher, codes, code_units(width, codes, flops[0]), ids)


def merged(many):
    top_s, top_t = jnp.max(many[:, 0], axis=0), jnp.max(many[:, 1], axis=0)
    fs, ft = jnp.exp(many[:, 0] - top_s), jnp.exp(many[:, 1] - top_t)
    return [
        top_s,
        top_t,
        jnp.sum(many[:, 2] * fs, axis=0),
        jnp.sum(many[:, 3] * ft, axis=0),
        jnp.sum(many[:, 4] * fs, axis=0),
        jnp.sum(many[:, 5] * fs, axis=0),
        jnp.sum(many[:, 6], axis=0),
        jnp.sum(many[:, 7], axis=0),
    ]


def merge_kernel(many, out):
    out[...] = jnp.stack(merged(many[...]))


def all_stats(stats):
    many = lax.all_to_all(stats, ("y", "x"), 0, 0)
    plane = pl.pallas_call(
        merge_kernel,
        in_specs=[VMEM],
        out_specs=VMEM,
        out_shape=jax.ShapeDtypeStruct(many.shape[1:], F32),
        compiler_params=params(4),
        cost_estimate=FREE,
    )(many)
    return [plane] + [rotate(plane, "z", 4, k) for k in (1, 2, 3)]


def grad_kernel(width, place, s0, s1, s2, s3, sl_ref, tl_ref, ids, grad, column):
    for k, got in enumerate((s0, s1, s2, s3)):
        column[(place[1] + 4 - k) % 4] = got[...]
    m = merged(column[...])
    top_s, top_t, total_s, total_t, weighted_s, weighted_t, pick_s, pick_t = (
        v.reshape(1, LANES) for v in m
    )
    norm_s = top_s + jnp.log(total_s)
    norm_t = top_t + jnp.log(total_t)
    divergence = FACTOR * (weighted_s / total_s - norm_s) - (weighted_t / total_s - norm_t)
    advantage = jnp.clip(pick_t - norm_t - (pick_s - norm_s), -ADVANTAGE_CLIP, ADVANTAGE_CLIP)
    loss = divergence - advantage * (pick_s - norm_s)
    sl, tl = sl_ref[...], tl_ref[...]
    row = lax.broadcasted_iota(jnp.int32, sl.shape, 0)
    onehot = row == ids[...] - place[0] * width
    probs = jnp.exp(sl - top_s) * (1.0 / total_s)
    inner = FACTOR * (sl - norm_s) - (tl - norm_t) - divergence
    out = probs * inner - advantage * (onehot.astype(F32) - probs)

    full = width // 16 * 16
    parts = []
    for _ in range(3):
        parts.append(loss.astype(BF16).astype(F32))
        loss = loss - parts[-1]
    blank = jnp.zeros((grad.shape[0] - width - 3, LANES), F32)
    grad[:full] = out[:full].astype(BF16)
    grad[full:] = jnp.concatenate([out[full:], *parts, blank], axis=0).astype(BF16)


def logit_grad(place, column, sl, tl, ids):
    width = sl.shape[0]
    rows = (width + 3 + 15) // 16 * 16
    return pl.pallas_call(
        functools.partial(grad_kernel, width),
        in_specs=[SMEM] + [VMEM] * 7,
        out_specs=VMEM,
        out_shape=jax.ShapeDtypeStruct((rows, LANES), BF16),
        scratch_shapes=[pltpu.VMEM((4, 8, LANES), F32)],
        compiler_params=params(16),
        cost_estimate=FREE,
    )(place, *column, sl, tl, ids)


def hidden_kernel(place, *refs):
    grads, w, out = refs[:-2], refs[-2], refs[-1]
    width, depth = w.shape
    for n, g in enumerate(grads):
        part = lax.dot_general(
            g[:width], w[...], (((0,), (0,)), ((), ())), preferred_element_type=F32
        )
        first = 8 * (place[2] ^ (n % 2))
        rows = pl.ds(16 * (n // 2), 16)
        out[pl.ds(first, 8), rows] = part.reshape(8, 16, depth).astype(BF16)


def hidden_part(place, pairs, w, flops):
    depth, n = w.shape[1], len(pairs)
    return pl.pallas_call(
        hidden_kernel,
        in_specs=[SMEM] + [VMEM] * (2 * n + 1),
        out_specs=VMEM,
        out_shape=jax.ShapeDtypeStruct((16, 16 * n, depth), BF16),
        compiler_params=params(24),
        cost_estimate=estimate(flops),
    )(place, *[v for pair in pairs for v in pair], w)


def scatter(part):
    return lax.all_to_all(part, ("y", "x"), 0, 0)


def summed(parts):
    got = jnp.sum(parts.astype(F32), axis=0)
    return got.reshape(-1, 16, got.shape[1])


def weight_kernel(loss_row, _, *refs):
    g = jnp.concatenate([r[...] for r in refs[:8]], axis=1)
    h = jnp.concatenate([r[...] for r in refs[8:16]], axis=0)
    refs[16][...] = jnp.dot(g, h, preferred_element_type=F32).astype(BF16)

    @pl.when(pl.program_id(0) == pl.num_programs(0) - 1)
    def _():
        first = loss_row // 16 * 16
        ends = [r[first : first + 16].astype(F32) for r in refs[:8]]
        at = loss_row - first
        v = [(e[at : at + 1] + e[at + 1 : at + 2]) + e[at + 2 : at + 3] for e in ends]
        near = (v[0] + v[1]) + (v[4] + v[5])
        far = (v[2] + v[3]) + (v[6] + v[7])
        refs[17][...] = jnp.broadcast_to(near + far, refs[17].shape)


def weight_grad(width, grads, hidden, blocks):
    depth = hidden.shape[1]
    block = 256
    loss_row = width % block
    assert loss_row + 3 <= block

    def rows(d):
        return pl.BlockSpec((block, d), lambda i, sc: (i, 0))

    def owned(k):
        return pl.BlockSpec((LANES, depth), lambda i, sc: (sc[k], 0))

    return pl.pallas_call(
        functools.partial(weight_kernel, loss_row),
        grid_spec=pltpu.PrefetchScalarGridSpec(
            num_scalar_prefetch=1,
            grid=(pl.cdiv(width, block),),
            in_specs=[rows(LANES)] * 8 + [owned(k) for k in range(8)],
            out_specs=[rows(depth), pl.BlockSpec((8, LANES), lambda i, sc: (0, 0))],
        ),
        out_shape=[
            jax.ShapeDtypeStruct((width, depth), BF16),
            jax.ShapeDtypeStruct((8, LANES), F32),
        ],
        compiler_params=params(24),
        cost_estimate=pl.CostEstimate(
            flops=16 * LANES * width * depth, bytes_accessed=4 * width * depth, transcendentals=0
        ),
    )(blocks, *grads, *([hidden] * 8))


def shards(teacher_hidden, teacher_weight, student_hidden, student_weight, rollout_ids):
    g, s, z = lax.axis_index("g"), lax.axis_index("s"), lax.axis_index("z")
    index = (z * 4 + lax.axis_index("y")) * 4 + lax.axis_index("x")
    place = jnp.stack([index, z, s]).astype(jnp.int32)
    tokens, depth = student_hidden.shape
    wt, ws = teacher_weight.T, student_weight.T
    width = ws.shape[0]

    def block_of(c, gr, sr):
        return 4 * (g ^ gr) + 2 * c + (s ^ sr)

    blocks = jnp.stack(
        [block_of(c, gr, sr) for c in range(2) for gr in range(2) for sr in range(2)]
    ).astype(jnp.int32)

    def core_sums(grp, core):
        give_s = swap(partial_logits(ws, student_hidden, grp, 1 - core), "s")
        give_t = swap(partial_logits(wt, teacher_hidden, grp, 1 - core), "s")
        keep_s = partial_logits(ws, student_hidden, grp, core)
        keep_t = partial_logits(wt, teacher_hidden, grp, core)
        return (keep_s, give_s), (keep_t, give_t)

    here = rollout_ids.reshape(2, LANES)
    other = swap(lax.dynamic_index_in_dim(here, 1 - s, 0, keepdims=True), "s")
    mine = lax.dynamic_index_in_dim(here, s, 0, keepdims=True)
    ids = [jnp.where(s == c, mine, other) for c in range(2)]

    codes0, codes1 = encode(*core_sums(1 - g, s))
    far0 = swap(codes0, "g")
    near_blocks = jnp.stack([block_of(c, 0, sr) for sr in range(2) for c in range(2)])
    keep_s, give_s, keep_t, give_t = near_logits(
        ordered(near_blocks.astype(jnp.int32), codes0), student_hidden, teacher_hidden, ws, wt
    )
    near = (keep_s, swap(give_s, "s")), (keep_t, swap(give_t, "s"))
    far1 = swap(ordered(codes1, far0), "g")
    sl0, tl0, stats0 = local_stats(place, 0, *near, far0, (HIDES, 1), ids[0])
    grad0 = logit_grad(place, all_stats(stats0), sl0, tl0, ids[0])
    away0 = swap(grad0, "g")
    sl1, tl1, stats1 = local_stats(place, 1, *near, far1, (1, SECOND), ordered(ids[1], grad0))
    grad1 = logit_grad(place, all_stats(stats1), sl1, tl1, ids[1])
    away1 = swap(ordered(grad1, away0), "g")
    after = (grad0, ordered(away0, grad1), grad1, away1)
    pairs = [(v, swap(v, "s")) for v in after]
    early = scatter(hidden_part(place, pairs[:2], ws, 1))
    part = hidden_part(place, pairs[2:], ws, LAST)
    late = scatter(ordered(part, early))
    grads = [v for pair in pairs for v in pair]
    grad_weight, losses = weight_grad(width, grads, student_hidden, ordered(blocks, part))
    late = ordered(late, losses)
    sums = jnp.concatenate([summed(early), summed(late)], axis=0)

    def block(dest):
        return lax.dynamic_index_in_dim(
            sums, 2 * (dest % 2) + (g ^ (dest // 2)), 0, keepdims=False
        )

    total = block(z)
    for k in (1, 2, 3):
        total = total + rotate(block((z + k) % 4), "z", 4, k)
    return total.astype(BF16), grad_weight.T, jnp.sum(losses[0]) / tokens


def solution(mesh):
    split = Mesh(mesh.devices.reshape(2, 2, 4, 4, 4), ("g", "s", "z", "y", "x"))
    owners, vocab = ("g", "s"), ("z", "y", "x")
    return jax.shard_map(
        shards,
        mesh=split,
        in_specs=(P(None, owners), P(owners, vocab), P(None, owners), P(owners, vocab), P(owners)),
        out_specs=(P(vocab, owners), P(owners, vocab), P()),
        check_vma=False,
    )
```

time: 192 us -> 179 us (0.932)
  matrix products: 22.5 us -> 5.64 us
  local copies, waits for them, and re-layouts: 11.2 us -> 17.5 us
  blocking collectives: 31.9 us -> 37.7 us
  Pallas kernels: 21.4 us -> 26.2 us
  other arithmetic: 8.36 us -> 4.5 us
  between operations: 5.96 us -> 2.86 us
  starting transfers between devices: 40.3 us -> 37.3 us
    ppermute x8 -> x13, waiting for transfers between devices: 35.9 us -> 16.3 us  [swap(): return lax.ppermute(x, axis, [(0, 1), (1, 0)])]
    dot_general x8 -> x4, matrix products: 22.5 us -> 5.64 us  [partial_logits(): lax.dot_general(weight, rows, (((1,), (1,)), ((), ())), preferred_element...]
    ppermute x6 -> x9, waiting for transfers between devices: 4.29 us -> 14.5 us  [rotate(): return lax.ppermute(x, axis, [(i, (i + step) % size) for i in range(size)])]
    ppermute x6 -> x9, starting transfers between devices: 19.4 us -> 10 us  [rotate(): return lax.ppermute(x, axis, [(i, (i + step) % size) for i in range(size)])]
    all_to_all x2, waiting for transfers between devices: 6.7 us -> 14.2 us  [scatter(): return lax.all_to_all(part, ('y', 'x'), 0, 0)]
    ppermute x8 -> x13, starting transfers between devices: 11.8 us -> 18.5 us  [swap(): return lax.ppermute(x, axis, [(0, 1), (1, 0)])]
    all_to_all x1 -> x2, blocking collectives: 31.9 us -> 37.7 us  [all_stats(): many = lax.all_to_all(stats, ('y', 'x'), 0, 0)]
    unnamed x26 -> x38, local copies, waits for them, and re-layouts: 10.6 us -> 16 us
  transfers between devices with their start and end apart: 16 -> 24, of which waited for: 10 -> 14; matrix products, arithmetic and copies ran while one was open for 13% -> 3% of each run, Pallas kernels for 7% -> 13%
where the time goes in v2:
time: 179 us; the launch traced here: 177 us
  waiting for transfers between devices  45 us (25%)
  blocking collectives  37.7 us (21%)
  starting transfers between devices  37.3 us (21%)
  Pallas kernels  26.2 us (15%)
  local copies, waits for them, and re-layouts  17.5 us (10%)
  matrix products  5.64 us (3%)
  other arithmetic  4.5 us (3%)
  between operations  2.86 us (2%)
    all_to_all x2, blocking collectives, all_stats(): many = lax.all_to_all(stats, ('y', 'x'), 0, 0)  37.7 us
    ppermute x13, starting transfers between devices, swap(): return lax.ppermute(x, axis, [(0, 1), (1, 0)])  18.5 us
    ppermute x13, waiting for transfers between devices, swap(): return lax.ppermute(x, axis, [(0, 1), (1, 0)])  16.3 us
    unnamed x38, local copies, waits for them, and re-layouts  16 us
    ppermute x9, waiting for transfers between devices, rotate(): return lax.ppermute(x, axis, [(i, (i + step) % size) for i in range(size)])  14.5 us
    all_to_all x2, waiting for transfers between devices, scatter(): return lax.all_to_all(part, ('y', 'x'), 0, 0)  14.2 us
    ppermute x9, starting transfers between devices, rotate(): return lax.ppermute(x, axis, [(i, (i + step) % size) for i in range(size)])  10 us
    all_to_all x2, starting transfers between devices, scatter(): return lax.all_to_all(part, ('y', 'x'), 0, 0)  8.77 us
  transfers between devices with their start and end apart: 24, of which 14 were waited for; matrix products, arithmetic and copies ran while one was open for 3% of the time, Pallas kernels for 13%

profile of v2, /device:TPU:0, one launch (start us, length us, event | category | flops | bytes accessed | tf_op | source)
XLA Modules:
  0.0 176.7 jit_solution(91527256271882215)
XLA Ops:
  1.9 2.7 %convolution_bitcast_fusion.2 = f32[1187,256]{1,0:T(8,128)S(1)} fusion(bf16[256,1024]{1,0:T(8,128)(2,1)S(1)} %bitcast.62, bf16[1024,1187]{0,1:T(8,128)(2,1)} %param.6), kind=kOutput, calls=%fused_computation.2 | convolution fusion | flops 622329856 | bytes 4170752 | tf_op jit(solution)/shard_map/dot_general | solution.py:51
  9.4 1.8 %shard_map.76 = (s16[2,1200,128]{2,1,0:T(8,128)(2,1)}, s16[2,1200,128]{2,1,0:T(8,128)(2,1)S(1)}) custom-call(f32[1187,256]{1,0:T(8,128)S(1)} %convolution_bitcast_fusion.1.as_, f32[1187,256]{1,0:T(8,128)S(1)} %collective-permute-done.bs, f32[1187,256]{1,0:T(8,128)S(1)} %convolution_bitcast_fusion.3.at, f32[1187,256]{1,0:T(8,128)S(1)} %collective-permute-done.1.bt), custom_call_target="tpu_custom_call" | custom-call | flops 153600 | bytes 3072000 | tf_op jit(solution)/shard_map/pallas_call | solution.py:117
  12.0 5.5 %collective-permute-start.4 = (s16[2,1200,128]{2,1,0:T(8,128)(2,1)}, s16[2,1200,128]{2,1,0:T(8,128)(2,1)S(1)}, u32[]{:S(2)}, u32[]{:S(2)}) collective-permute-start(s16[2,1200,128]{2,1,0:T(8,128)(2,1)} %get-tuple-element.25), channel_id=1, source_target_pairs={{0,128},{128,0},{1,129},{129,1},{2,130},{130,2},{3,131},{131,3},{4... | collective-permute-start | bytes 1843208 | tf_op jit(solution)/shard_map/ppermute | solution.py:36
  18.7 1.6 copy-done.1
  20.3 1.7 copy-done.3
  22.0 1.9 %copy-done.5 = bf16[1280,1187]{0,1:T(8,128)(2,1)S(1)} copy-done((bf16[1280,1187]{0,1:T(8,128)(2,1)S(1)}, bf16[1280,1187]{0,1:T(8,128)(2,1)}, u32[]{:S(2)}) %copy-start.5) | copy-done | bytes 3038744
  23.9 5.9 %shard_map.77 = (f32[1187,256]{1,0:T(8,128)S(1)}, f32[1187,256]{1,0:T(8,128)S(1)}, f32[1187,256]{1,0:T(8,128)S(1)}, f32[1187,256]{1,0:T(8,128)S(1)}) custom-call(s32[4]{0:T(128)S(1)} %pad_add_fusion.1._, bf16[1024,1280]{1,0:T(8,128)(2,1)S(1)} %copy-done, bf16[1024,1280]{1,0:T(8,128)(2,1)S(1)} %copy-done, bf16[1024,1280]{1,0:T(8,128)(2,1)S(1)} %copy-done, ...), custom_call_target="tpu_custom_call" | custom-call | flops 1 | bytes 1 | tf_op jit(solution)/shard_map/pallas_call | solution.py:81
  30.4 5.3 %collective-permute-done.4.codes = s16[2,1200,128]{2,1,0:T(8,128)(2,1)S(1)} collective-permute-done((s16[2,1200,128]{2,1,0:T(8,128)(2,1)}, s16[2,1200,128]{2,1,0:T(8,128)(2,1)S(1)}, u32[]{:S(2)}, u32[]{:S(2)}) %collective-permute-start.4) | collective-permute-done | bytes 614432 | tf_op jit(solution)/shard_map/ppermute | solution.py:36
  35.6 5.6 %collective-permute-start.11 = (s16[2,1200,128]{2,1,0:T(8,128)(2,1)S(1)}, s16[2,1200,128]{2,1,0:T(8,128)(2,1)S(1)}, u32[]{:S(2)}, u32[]{:S(2)}) collective-permute-start(s16[2,1200,128]{2,1,0:T(8,128)(2,1)S(1)} %copy-done.17), channel_id=1, source_target_pairs={{0,128},{128,0},{1,129},{129,1},{2,130},{130,2},{3,131},{131,3},{4... | collective-permute-start | bytes 1843208 | tf_op jit(solution)/shard_map/ppermute | solution.py:36
  42.7 23.4 %all_to_all.20.many = f32[16,8,128]{2,1,0:T(8,128)S(1)} all-to-all(f32[16,8,128]{2,1,0:T(8,128)S(1)} %get-tuple-element.31), channel_id=1, replica_groups=mesh['g'=2,'s'=2,'z'=4,'y'=4,'x'=4] {'y','x'}, dimensions={0} | all-to-all | bytes 131072 | tf_op jit(solution)/shard_map/all_to_all | solution.py:220
  66.3 3.1 %collective-permute-start.7 = (f32[8,128]{1,0:T(8,128)S(1)}, f32[8,128]{1,0:T(8,128)S(1)}, u32[]{:S(2)}, u32[]{:S(2)}) collective-permute-start(f32[8,128]{1,0:T(8,128)S(1)} %shard_map.80.s0), channel_id=1, source_target_pairs={{0,32},{16,48},{32,0},{48,16},{1,33},{17,49},{33,1},{49,17},{2,34}... | collective-permute-start | bytes 12296 | tf_op jit(solution)/shard_map/ppermute | solution.py:40
  70.3 5.5 %collective-permute-done.8.s3 = f32[8,128]{1,0:T(8,128)S(1)} collective-permute-done((f32[8,128]{1,0:T(8,128)S(1)}, f32[8,128]{1,0:T(8,128)S(1)}, u32[]{:S(2)}, u32[]{:S(2)}) %collective-permute-start.8) | collective-permute-done | bytes 4128 | tf_op jit(solution)/shard_map/ppermute | solution.py:40
  78.5 4.2 %collective-permute-start.10 = (bf16[1200,128]{1,0:T(8,128)(2,1)S(1)}, bf16[1200,128]{1,0:T(8,128)(2,1)S(1)}, u32[]{:S(2)}, u32[]{:S(2)}) collective-permute-start(bf16[1200,128]{1,0:T(8,128)(2,1)S(1)} %shard_map.81.refs_0_), channel_id=1, source_target_pairs={{0,128},{128,0},{1,129},{129,1},{2,130},{130,2},{3,131},{131,3},{4... | collective-permute-start | bytes 921608 | tf_op jit(solution)/shard_map/ppermute | solution.py:36
  84.1 14.3 %all_to_all.21.many = f32[16,8,128]{2,1,0:T(8,128)S(1)} all-to-all(f32[16,8,128]{2,1,0:T(8,128)S(1)} %get-tuple-element.37), channel_id=1, replica_groups=mesh['g'=2,'s'=2,'z'=4,'y'=4,'x'=4] {'y','x'}, dimensions={0} | all-to-all | bytes 131072 | tf_op jit(solution)/shard_map/all_to_all | solution.py:220
  98.5 2.0 %collective-permute-start.13 = (f32[8,128]{1,0:T(8,128)S(1)}, f32[8,128]{1,0:T(8,128)S(1)}, u32[]{:S(2)}, u32[]{:S(2)}) collective-permute-start(f32[8,128]{1,0:T(8,128)S(1)} %shard_map.84.s0), channel_id=1, source_target_pairs={{0,32},{16,48},{32,0},{48,16},{1,33},{17,49},{33,1},{49,17},{2,34}... | collective-permute-start | bytes 12296 | tf_op jit(solution)/shard_map/ppermute | solution.py:40
  100.5 1.6 collective-permute-done.14.s3
  103.1 2.8 %collective-permute-done.12.s1 = f32[8,128]{1,0:T(8,128)S(1)} collective-permute-done((f32[8,128]{1,0:T(8,128)S(1)}, f32[8,128]{1,0:T(8,128)S(1)}, u32[]{:S(2)}, u32[]{:S(2)}) %collective-permute-start.12) | collective-permute-done | bytes 4128 | tf_op jit(solution)/shard_map/ppermute | solution.py:40
  105.9 1.9 %shard_map.85.refs_0_.refs_4_ = bf16[1200,128]{1,0:T(8,128)(2,1)} custom-call(s32[3]{0:T(128)S(1)} %pad_add_fusion.place, f32[8,128]{1,0:T(8,128)S(1)} %shard_map.84.s0, f32[8,128]{1,0:T(8,128)S(1)} %collective-permute-done.12.s1, f32[8,128]{1,0:T(8,128)S(1)} %collective-permute-done.13.s2, f32[8,128]{1,0:T(8,128)S(1)} %collective-permute-done.14.s3, ...), custom_call_target="tpu_custom_call" | custom-call | flops 1 | bytes 1 | tf_op jit(solution)/shard_map/pallas_call | solution.py:264
  107.9 2.0 %collective-permute-start.17 = (bf16[1200,128]{1,0:T(8,128)(2,1)}, bf16[1200,128]{1,0:T(8,128)(2,1)}, u32[]{:S(2)}, u32[]{:S(2)}) collective-permute-start(bf16[1200,128]{1,0:T(8,128)(2,1)} %shard_map.85.refs_0_.refs_4_), channel_id=1, source_target_pairs={{0,128},{128,0},{1,129},{129,1},{2,130},{130,2},{3,131},{131,3},{4... | collective-permute-start | bytes 921608 | tf_op jit(solution)/shard_map/ppermute | solution.py:36
  109.8 2.5 %shard_map.86 = bf16[16,32,1280]{2,1,0:T(8,128)(2,1)S(1)} custom-call(s32[3]{0:T(128)S(1)} %pad_add_fusion.place, bf16[1200,128]{1,0:T(8,128)(2,1)S(1)} %shard_map.81.refs_0_, bf16[1200,128]{1,0:T(8,128)(2,1)S(1)} %collective-permute-done.9.refs_1_, bf16[1200,128]{1,0:T(8,128)(2,1)S(1)} %collective-permute-done.10.refs_2_, ...), custom_call_target="tpu_custom_call" | custom-call | flops 1 | bytes 1 | tf_op jit(solution)/shard_map/pallas_call | solution.py:289
  114.1 4.4 %all-to-all-start.2 = ((bf16[16,32,1280]{2,1,0:T(8,128)(2,1)}), bf16[16,32,1280]{2,1,0:T(8,128)(2,1)}, u32[]{:S(2)}, u32[]{:S(2)}) async-start(bf16[16,32,1280]{2,1,0:T(8,128)(2,1)} %copy-done.8), calls=%async_computation.2 | async-start | bytes 2621440 | tf_op jit(solution)/shard_map/all_to_all | solution.py:300
  118.8 7.9 %collective-permute-done.17.refs_2_.refs_6_ = bf16[1200,128]{1,0:T(8,128)(2,1)} collective-permute-done((bf16[1200,128]{1,0:T(8,128)(2,1)}, bf16[1200,128]{1,0:T(8,128)(2,1)}, u32[]{:S(2)}, u32[]{:S(2)}) %collective-permute-start.17) | collective-permute-done | bytes 307232 | tf_op jit(solution)/shard_map/ppermute | solution.py:36
  126.8 1.7 collective-permute-done.18.refs_3_.refs_7_
  128.6 1.9 %copy-done.7 = bf16[1280,1187]{0,1:T(8,128)(2,1)S(1)} copy-done((bf16[1280,1187]{0,1:T(8,128)(2,1)S(1)}, bf16[1280,1187]{0,1:T(8,128)(2,1)}, u32[]{:S(2)}) %copy-start.7) | copy-done | bytes 3038744
  130.4 3.0 %shard_map.87 = bf16[16,32,1280]{2,1,0:T(8,128)(2,1)S(1)} custom-call(s32[3]{0:T(128)S(1)} %pad_add_fusion.place, bf16[1200,128]{1,0:T(8,128)(2,1)} %shard_map.85.refs_0_.refs_4_, bf16[1200,128]{1,0:T(8,128)(2,1)S(1)} %collective-permute-done.16.refs_1_.refs_5_, bf16[1200,128]{1,0:T(8,128)(2,1)} %collective-permute-done.17.refs_2_.refs_6_, ...), custom_call_target="tpu_custom_call" | custom-call | flops 8200000000 | bytes 1 | tf_op jit(solution)/shard_map/pallas_call | solution.py:289
  136.0 5.0 %all-to-all-done.2 = bf16[16,32,1280]{2,1,0:T(8,128)(2,1)} async-done(((bf16[16,32,1280]{2,1,0:T(8,128)(2,1)}), bf16[16,32,1280]{2,1,0:T(8,128)(2,1)}, u32[]{:S(2)}, u32[]{:S(2)}) %all-to-all-start.2) | async-done | bytes 1310752 | tf_op jit(solution)/shard_map/all_to_all | solution.py:300
  141.0 4.4 %all-to-all-start.3 = ((bf16[16,32,1280]{2,1,0:T(8,128)(2,1)}), bf16[16,32,1280]{2,1,0:T(8,128)(2,1)}, u32[]{:S(2)}, u32[]{:S(2)}) async-start(bf16[16,32,1280]{2,1,0:T(8,128)(2,1)} %copy-done.9), calls=%async_computation.3 | async-start | bytes 2621440 | tf_op jit(solution)/shard_map/all_to_all | solution.py:300
  148.6 6.8 %shard_map.88 = (bf16[1187,1280]{1,0:T(8,128)(2,1)}, f32[8,128]{1,0:T(8,128)S(1)}) custom-call(s32[8]{0:T(128)S(1)} %stack.59._, bf16[1200,128]{1,0:T(8,128)(2,1)S(1)} %shard_map.81.refs_0_, bf16[1200,128]{1,0:T(8,128)(2,1)S(1)} %collective-permute-done.9.refs_1_, bf16[1200,128]{1,0:T(8,128)(2,1)S(1)} %collective-permute-done.10.refs_2_, ...), custom_call_target="tpu_custom_call" | custom-call | flops 3111649280 | bytes 6077440 | tf_op jit(solution)/shard_map/pallas_call | solution.py:336
  155.4 1.5 convert_reduce_fusion.1
  156.9 9.2 %all-to-all-done.3 = bf16[16,32,1280]{2,1,0:T(8,128)(2,1)} async-done(((bf16[16,32,1280]{2,1,0:T(8,128)(2,1)}), bf16[16,32,1280]{2,1,0:T(8,128)(2,1)}, u32[]{:S(2)}, u32[]{:S(2)}) %all-to-all-start.3) | async-done | bytes 1310752 | tf_op jit(solution)/shard_map/all_to_all | solution.py:300
  166.0 1.5 convert_reduce_fusion
  168.9 2.6 %collective-permute-start.21 = (f32[16,1280]{1,0:T(8,128)S(1)}, f32[16,1280]{1,0:T(8,128)S(1)}, u32[]{:S(2)}, u32[]{:S(2)}) collective-permute-start(f32[16,1280]{1,0:T(8,128)S(1)} %get-tuple-element.53), channel_id=1, source_target_pairs={{0,48},{16,0},{32,16},{48,32},{1,49},{17,1},{33,17},{49,33},{2,50}... | collective-permute-start | bytes 245768 | tf_op jit(solution)/shard_map/ppermute | solution.py:40
  (85 shorter events, 28.7 us)
Async XLA Ops:
  1.9 2.8 %copy-start = (bf16[1024,1280]{1,0:T(8,128)(2,1)S(1)}, bf16[1024,1280]{1,0:T(8,128)(2,1)}, u32[]{:S(2)}) copy-start(bf16[1024,1280]{1,0:T(8,128)(2,1)} %refs_15_.1) | copy-start | bytes 7864324
  1.9 3.4 %copy-start.4 = (bf16[1280,1187]{0,1:T(8,128)(2,1)S(1)}, bf16[1280,1187]{0,1:T(8,128)(2,1)}, u32[]{:S(2)}) copy-start(bf16[1280,1187]{0,1:T(8,128)(2,1)} %param.8) | copy-start | bytes 9116164
  4.6 4.3 %collective-permute-start.1 = (f32[1187,256]{1,0:T(8,128)S(1)}, f32[1187,256]{1,0:T(8,128)S(1)}, u32[]{:S(2)}, u32[]{:S(2)}) collective-permute-start(f32[1187,256]{1,0:T(8,128)S(1)} %convolution_bitcast_fusion.2), channel_id=1, source_target_pairs={{0,64},{64,0},{1,65},{65,1},{2,66},{66,2},{3,67},{67,3},{4,68},{68... | collective-permute-start | bytes 3646472 | tf_op jit(solution)/shard_map/ppermute | solution.py:36
  6.4 3.0 %collective-permute-start = (f32[1187,256]{1,0:T(8,128)S(1)}, f32[1187,256]{1,0:T(8,128)S(1)}, u32[]{:S(2)}, u32[]{:S(2)}) collective-permute-start(f32[1187,256]{1,0:T(8,128)S(1)} %convolution_bitcast_fusion), channel_id=1, source_target_pairs={{0,64},{64,0},{1,65},{65,1},{2,66},{66,2},{3,67},{67,3},{4,68},{68... | collective-permute-start | bytes 3646472 | tf_op jit(solution)/shard_map/ppermute | solution.py:36
  8.9 8.6 %copy-start.18 = (s32[256]{0:T(256)S(1)}, s32[256]{0:T(256)}, u32[]{:S(2)}) copy-start(s32[256]{0:T(256)} %param.9) | copy-start | bytes 3076
  12.0 23.6 %collective-permute-start.4 = (s16[2,1200,128]{2,1,0:T(8,128)(2,1)}, s16[2,1200,128]{2,1,0:T(8,128)(2,1)S(1)}, u32[]{:S(2)}, u32[]{:S(2)}) collective-permute-start(s16[2,1200,128]{2,1,0:T(8,128)(2,1)} %get-tuple-element.25), channel_id=1, source_target_pairs={{0,128},{128,0},{1,129},{129,1},{2,130},{130,2},{3,131},{131,3},{4... | collective-permute-start | bytes 1843208 | tf_op jit(solution)/shard_map/ppermute | solution.py:36
  17.5 1.2 collective-permute-start.5
  20.3 1.7 copy-start.3
  22.0 1.9 %copy-start.5 = (bf16[1280,1187]{0,1:T(8,128)(2,1)S(1)}, bf16[1280,1187]{0,1:T(8,128)(2,1)}, u32[]{:S(2)}) copy-start(bf16[1280,1187]{0,1:T(8,128)(2,1)} %param.8) | copy-start | bytes 9116164
  23.9 11.8 %copy-start.17 = (s16[2,1200,128]{2,1,0:T(8,128)(2,1)S(1)}, s16[2,1200,128]{2,1,0:T(8,128)(2,1)}, u32[]{:S(2)}) copy-start(s16[2,1200,128]{2,1,0:T(8,128)(2,1)} %copy-done.16) | copy-start | bytes 1843204
  29.8 11.5 %collective-permute-start.2 = (f32[1187,256]{1,0:T(8,128)S(1)}, f32[1187,256]{1,0:T(8,128)S(1)}, u32[]{:S(2)}, u32[]{:S(2)}) collective-permute-start(f32[1187,256]{1,0:T(8,128)S(1)} %get-tuple-element.28), channel_id=1, source_target_pairs={{0,64},{64,0},{1,65},{65,1},{2,66},{66,2},{3,67},{67,3},{4,68},{68... | collective-permute-start | bytes 3646472 | tf_op jit(solution)/shard_map/ppermute | solution.py:36
  30.1 11.2 %collective-permute-start.3 = (f32[1187,256]{1,0:T(8,128)S(1)}, f32[1187,256]{1,0:T(8,128)S(1)}, u32[]{:S(2)}, u32[]{:S(2)}) collective-permute-start(f32[1187,256]{1,0:T(8,128)S(1)} %get-tuple-element.30), channel_id=1, source_target_pairs={{0,64},{64,0},{1,65},{65,1},{2,66},{66,2},{3,67},{67,3},{4,68},{68... | collective-permute-start | bytes 3646472 | tf_op jit(solution)/shard_map/ppermute | solution.py:36
  35.6 34.6 %collective-permute-start.11 = (s16[2,1200,128]{2,1,0:T(8,128)(2,1)S(1)}, s16[2,1200,128]{2,1,0:T(8,128)(2,1)S(1)}, u32[]{:S(2)}, u32[]{:S(2)}) collective-permute-start(s16[2,1200,128]{2,1,0:T(8,128)(2,1)S(1)} %copy-done.17), channel_id=1, source_target_pairs={{0,128},{128,0},{1,129},{129,1},{2,130},{130,2},{3,131},{131,3},{4... | collective-permute-start | bytes 1843208 | tf_op jit(solution)/shard_map/ppermute | solution.py:36
  66.2 9.5 %collective-permute-start.8 = (f32[8,128]{1,0:T(8,128)S(1)}, f32[8,128]{1,0:T(8,128)S(1)}, u32[]{:S(2)}, u32[]{:S(2)}) collective-permute-start(f32[8,128]{1,0:T(8,128)S(1)} %shard_map.80.s0), channel_id=1, source_target_pairs={{0,48},{16,0},{32,16},{48,32},{1,49},{17,1},{33,17},{49,33},{2,50}... | collective-permute-start | bytes 12296 | tf_op jit(solution)/shard_map/ppermute | solution.py:40
  66.3 11.0 %collective-permute-start.7 = (f32[8,128]{1,0:T(8,128)S(1)}, f32[8,128]{1,0:T(8,128)S(1)}, u32[]{:S(2)}, u32[]{:S(2)}) collective-permute-start(f32[8,128]{1,0:T(8,128)S(1)} %shard_map.80.s0), channel_id=1, source_target_pairs={{0,32},{16,48},{32,0},{48,16},{1,33},{17,49},{33,1},{49,17},{2,34}... | collective-permute-start | bytes 12296 | tf_op jit(solution)/shard_map/ppermute | solution.py:40
  69.4 7.9 %collective-permute-start.6 = (f32[8,128]{1,0:T(8,128)S(1)}, f32[8,128]{1,0:T(8,128)S(1)}, u32[]{:S(2)}, u32[]{:S(2)}) collective-permute-start(f32[8,128]{1,0:T(8,128)S(1)} %shard_map.80.s0), channel_id=1, source_target_pairs={{0,16},{16,32},{32,48},{48,0},{1,17},{17,33},{33,49},{49,1},{2,18}... | collective-permute-start | bytes 12296 | tf_op jit(solution)/shard_map/ppermute | solution.py:40
  78.5 29.4 %collective-permute-start.10 = (bf16[1200,128]{1,0:T(8,128)(2,1)S(1)}, bf16[1200,128]{1,0:T(8,128)(2,1)S(1)}, u32[]{:S(2)}, u32[]{:S(2)}) collective-permute-start(bf16[1200,128]{1,0:T(8,128)(2,1)S(1)} %shard_map.81.refs_0_), channel_id=1, source_target_pairs={{0,128},{128,0},{1,129},{129,1},{2,130},{130,2},{3,131},{131,3},{4... | collective-permute-start | bytes 921608 | tf_op jit(solution)/shard_map/ppermute | solution.py:36
  82.6 27.2 %copy-start.6 = (bf16[1280,1187]{0,1:T(8,128)(2,1)S(1)}, bf16[1280,1187]{0,1:T(8,128)(2,1)}, u32[]{:S(2)}) copy-start(bf16[1280,1187]{0,1:T(8,128)(2,1)} %param.8) | copy-start | bytes 9116164
  98.4 3.7 %collective-permute-start.14 = (f32[8,128]{1,0:T(8,128)S(1)}, f32[8,128]{1,0:T(8,128)S(1)}, u32[]{:S(2)}, u32[]{:S(2)}) collective-permute-start(f32[8,128]{1,0:T(8,128)S(1)} %shard_map.84.s0), channel_id=1, source_target_pairs={{0,48},{16,0},{32,16},{48,32},{1,49},{17,1},{33,17},{49,33},{2,50}... | collective-permute-start | bytes 12296 | tf_op jit(solution)/shard_map/ppermute | solution.py:40
  98.5 4.6 %collective-permute-start.13 = (f32[8,128]{1,0:T(8,128)S(1)}, f32[8,128]{1,0:T(8,128)S(1)}, u32[]{:S(2)}, u32[]{:S(2)}) collective-permute-start(f32[8,128]{1,0:T(8,128)S(1)} %shard_map.84.s0), channel_id=1, source_target_pairs={{0,32},{16,48},{32,0},{48,16},{1,33},{17,49},{33,1},{49,17},{2,34}... | collective-permute-start | bytes 12296 | tf_op jit(solution)/shard_map/ppermute | solution.py:40
  100.5 5.4 %collective-permute-start.12 = (f32[8,128]{1,0:T(8,128)S(1)}, f32[8,128]{1,0:T(8,128)S(1)}, u32[]{:S(2)}, u32[]{:S(2)}) collective-permute-start(f32[8,128]{1,0:T(8,128)S(1)} %shard_map.84.s0), channel_id=1, source_target_pairs={{0,16},{16,32},{32,48},{48,0},{1,17},{17,33},{33,49},{49,1},{2,18}... | collective-permute-start | bytes 12296 | tf_op jit(solution)/shard_map/ppermute | solution.py:40
  100.5 9.3 %collective-permute-start.9 = (bf16[1200,128]{1,0:T(8,128)(2,1)S(1)}, bf16[1200,128]{1,0:T(8,128)(2,1)S(1)}, u32[]{:S(2)}, u32[]{:S(2)}) collective-permute-start(bf16[1200,128]{1,0:T(8,128)(2,1)S(1)} %shard_map.81.refs_0_), channel_id=1, source_target_pairs={{0,64},{64,0},{1,65},{65,1},{2,66},{66,2},{3,67},{67,3},{4,68},{68... | collective-permute-start | bytes 921608 | tf_op jit(solution)/shard_map/ppermute | solution.py:36
  107.8 2.0 %collective-permute-start.15 = (bf16[1200,128]{1,0:T(8,128)(2,1)S(1)}, bf16[1200,128]{1,0:T(8,128)(2,1)S(1)}, u32[]{:S(2)}, u32[]{:S(2)}) collective-permute-start(bf16[1200,128]{1,0:T(8,128)(2,1)S(1)} %collective-permute-done.10.refs_2_), channel_id=1, source_target_pairs={{0,64},{64,0},{1,65},{65,1},{2,66},{66,2},{3,67},{67,3},{4,68},{68... | collective-permute-start | bytes 921608 | tf_op jit(solution)/shard_map/ppermute | solution.py:36
  107.9 18.9 %collective-permute-start.17 = (bf16[1200,128]{1,0:T(8,128)(2,1)}, bf16[1200,128]{1,0:T(8,128)(2,1)}, u32[]{:S(2)}, u32[]{:S(2)}) collective-permute-start(bf16[1200,128]{1,0:T(8,128)(2,1)} %shard_map.85.refs_0_.refs_4_), channel_id=1, source_target_pairs={{0,128},{128,0},{1,129},{129,1},{2,130},{130,2},{3,131},{131,3},{4... | collective-permute-start | bytes 921608 | tf_op jit(solution)/shard_map/ppermute | solution.py:36
  114.1 26.9 %all-to-all-start.2 = ((bf16[16,32,1280]{2,1,0:T(8,128)(2,1)}), bf16[16,32,1280]{2,1,0:T(8,128)(2,1)}, u32[]{:S(2)}, u32[]{:S(2)}) async-start(bf16[16,32,1280]{2,1,0:T(8,128)(2,1)} %copy-done.8), calls=%async_computation.2 | async-start | bytes 2621440 | tf_op jit(solution)/shard_map/all_to_all | solution.py:300
  118.5 8.3 %collective-permute-start.16 = (bf16[1200,128]{1,0:T(8,128)(2,1)}, bf16[1200,128]{1,0:T(8,128)(2,1)S(1)}, u32[]{:S(2)}, u32[]{:S(2)}) collective-permute-start(bf16[1200,128]{1,0:T(8,128)(2,1)} %shard_map.85.refs_0_.refs_4_), channel_id=1, source_target_pairs={{0,64},{64,0},{1,65},{65,1},{2,66},{66,2},{3,67},{67,3},{4,68},{68... | collective-permute-start | bytes 921608 | tf_op jit(solution)/shard_map/ppermute | solution.py:36
  126.8 1.8 %collective-permute-start.18 = (bf16[1200,128]{1,0:T(8,128)(2,1)}, bf16[1200,128]{1,0:T(8,128)(2,1)S(1)}, u32[]{:S(2)}, u32[]{:S(2)}) collective-permute-start(bf16[1200,128]{1,0:T(8,128)(2,1)} %collective-permute-done.17.refs_2_.refs_6_), channel_id=1, source_target_pairs={{0,64},{64,0},{1,65},{65,1},{2,66},{66,2},{3,67},{67,3},{4,68},{68... | collective-permute-start | bytes 921608 | tf_op jit(solution)/shard_map/ppermute | solution.py:36
  128.6 1.9 %copy-start.7 = (bf16[1280,1187]{0,1:T(8,128)(2,1)S(1)}, bf16[1280,1187]{0,1:T(8,128)(2,1)}, u32[]{:S(2)}) copy-start(bf16[1280,1187]{0,1:T(8,128)(2,1)} %param.8) | copy-start | bytes 9116164
  141.0 25.0 %all-to-all-start.3 = ((bf16[16,32,1280]{2,1,0:T(8,128)(2,1)}), bf16[16,32,1280]{2,1,0:T(8,128)(2,1)}, u32[]{:S(2)}, u32[]{:S(2)}) async-start(bf16[16,32,1280]{2,1,0:T(8,128)(2,1)} %copy-done.9), calls=%async_computation.3 | async-start | bytes 2621440 | tf_op jit(solution)/shard_map/all_to_all | solution.py:300
  167.6 6.4 %collective-permute-start.19 = (f32[16,1280]{1,0:T(8,128)S(1)}, f32[16,1280]{1,0:T(8,128)S(1)}, u32[]{:S(2)}, u32[]{:S(2)}) collective-permute-start(f32[16,1280]{1,0:T(8,128)S(1)} %get-tuple-element.51), channel_id=1, source_target_pairs={{0,16},{16,32},{32,48},{48,0},{1,17},{17,33},{33,49},{49,1},{2,18}... | collective-permute-start | bytes 245768 | tf_op jit(solution)/shard_map/ppermute | solution.py:40
  167.7 6.3 %collective-permute-start.20 = (f32[16,1280]{1,0:T(8,128)S(1)}, f32[16,1280]{1,0:T(8,128)S(1)}, u32[]{:S(2)}, u32[]{:S(2)}) collective-permute-start(f32[16,1280]{1,0:T(8,128)S(1)} %get-tuple-element.52), channel_id=1, source_target_pairs={{0,32},{16,48},{32,0},{48,16},{1,33},{17,49},{33,1},{49,17},{2,34}... | collective-permute-start | bytes 245768 | tf_op jit(solution)/shard_map/ppermute | solution.py:40
  168.9 6.0 %collective-permute-start.21 = (f32[16,1280]{1,0:T(8,128)S(1)}, f32[16,1280]{1,0:T(8,128)S(1)}, u32[]{:S(2)}, u32[]{:S(2)}) collective-permute-start(f32[16,1280]{1,0:T(8,128)S(1)} %get-tuple-element.53), channel_id=1, source_target_pairs={{0,48},{16,0},{32,16},{48,32},{1,49},{17,1},{33,17},{49,33},{2,50}... | collective-permute-start | bytes 245768 | tf_op jit(solution)/shard_map/ppermute | solution.py:40
  (11 other events, 11.3 us)

commit v3 on v2

--- a/solution.py
+++ b/solution.py
@@ -93,36 +93,33 @@
     )(blocks, *([hidden_s] * 4), *([hidden_t] * 4), ws, wt)
 
 
-def code_kernel(width, as_, bs, at, bt, *codes):
+def code_kernel(width, as_, bs, at, bt, out):
     def put(v):
         return v.astype(jnp.int32).astype(jnp.int16)
 
     full = width // 16 * 16
-    blank = jnp.zeros((codes[0].shape[1] - width - 1, LANES), F32)
-    for c, out in enumerate(codes):
-        lanes = slice(c * LANES, (c + 1) * LANES)
-        for head, (a, b) in enumerate(((as_, bs), (at, bt))):
-            x = a[:, lanes] + b[:, lanes]
-            peak = jnp.max(jnp.abs(x), axis=0, keepdims=True)
-            power = jnp.ceil(jnp.log2(jnp.maximum(peak, 1e-30) / LEVELS) * 256.0)
-            scale = 1.0 / jnp.exp2(power * (1.0 / 256.0))
-            code = jnp.clip(jnp.round(x * scale), -32767.0, 32767.0)
-            out[head, :full] = put(code[:full])
-            out[head, full:] = put(jnp.concatenate([code[full:], power, blank], axis=0))
-
-
-def encode(student, teacher):
+    blank = jnp.zeros((out.shape[1] - width - 1, LANES), F32)
+    for head, (a, b) in enumerate(((as_, bs), (at, bt))):
+        x = a[...] + b[...]
+        peak = jnp.max(jnp.abs(x), axis=0, keepdims=True)
+        power = jnp.ceil(jnp.log2(jnp.maximum(peak, 1e-30) / LEVELS) * 256.0)
+        scale = 1.0 / jnp.exp2(power * (1.0 / 256.0))
+        code = jnp.clip(jnp.round(x * scale), -32767.0, 32767.0)
+        out[head, :full] = put(code[:full])
+        out[head, full:] = put(jnp.concatenate([code[full:], power, blank], axis=0))
+
+
+def encode(c, student, teacher):
     width = student[0].shape[0]
     rows = (width + 1 + 15) // 16 * 16
     return pl.pallas_call(
         functools.partial(code_kernel, width),
-        in_specs=[VMEM] * 4,
-        out_specs=[VMEM] * 2,
-        out_shape=[jax.ShapeDtypeStruct((2, rows, LANES), jnp.int16)] * 2,
+        grid=(1,),
+        in_specs=[pl.BlockSpec((width, LANES), lambda i: (0, c))] * 4,
+        out_specs=pl.BlockSpec((2, rows, LANES), lambda i: (0, 0, 0)),
+        out_shape=jax.ShapeDtypeStruct((2, rows, LANES), jnp.int16),
         compiler_params=params(16),
-        cost_estimate=pl.CostEstimate(
-            flops=rows * LANES, bytes_accessed=20 * rows * LANES, transcendentals=0
-        ),
+        cost_estimate=FREE,
     )(*student, *teacher)
 
 
@@ -379,11 +376,13 @@
     mine = lax.dynamic_index_in_dim(here, s, 0, keepdims=True)
     ids = [jnp.where(s == c, mine, other) for c in range(2)]
 
-    codes0, codes1 = encode(*core_sums(1 - g, s))
+    far_sums = core_sums(1 - g, s)
+    codes0 = encode(0, *far_sums)
     far0 = swap(codes0, "g")
+    codes1 = encode(1, *far_sums)
     near_blocks = jnp.stack([block_of(c, 0, sr) for sr in range(2) for c in range(2)])
     keep_s, give_s, keep_t, give_t = near_logits(
-        ordered(near_blocks.astype(jnp.int32), codes0), student_hidden, teacher_hidden, ws, wt
+        ordered(near_blocks.astype(jnp.int32), codes0, codes1), student_hidden, teacher_hidden, ws, wt
     )
     near = (keep_s, swap(give_s, "s")), (keep_t, swap(give_t, "s"))
     far1 = swap(ordered(codes1, far0), "g")

time: 179 us -> 178 us (level)
  waiting for transfers between devices: 45 us -> 40.7 us
  local copies, waits for them, and re-layouts: 17.5 us -> 20.3 us
    ppermute x13, waiting for transfers between devices: 16.3 us -> 12 us  [swap(): return lax.ppermute(x, axis, [(0, 1), (1, 0)])]
    unnamed x38 -> x50, local copies, waits for them, and re-layouts: 16 us -> 18.9 us
where the time goes in v3:
time: 178 us; the launch traced here: 176 us
  waiting for transfers between devices  40.7 us (23%)
  blocking collectives  37.7 us (21%)
  starting transfers between devices  37.4 us (21%)
  Pallas kernels  26.4 us (15%)
  local copies, waits for them, and re-layouts  20.3 us (11%)
  matrix products  5.61 us (3%)
  other arithmetic  4.5 us (3%)
  between operations  2.9 us (2%)
    all_to_all x2, blocking collectives, all_stats(): many = lax.all_to_all(stats, ('y', 'x'), 0, 0)  37.7 us
    unnamed x50, local copies, waits for them, and re-layouts  18.9 us
    ppermute x13, starting transfers between devices, swap(): return lax.ppermute(x, axis, [(0, 1), (1, 0)])  18.6 us
    ppermute x9, waiting for transfers between devices, rotate(): return lax.ppermute(x, axis, [(i, (i + step) % size) for i in range(size)])  14.5 us
    all_to_all x2, waiting for transfers between devices, scatter(): return lax.all_to_all(part, ('y', 'x'), 0, 0)  14.2 us
    ppermute x13, waiting for transfers between devices, swap(): return lax.ppermute(x, axis, [(0, 1), (1, 0)])  12 us
    ppermute x9, starting transfers between devices, rotate(): return lax.ppermute(x, axis, [(i, (i + step) % size) for i in range(size)])  10 us
    all_to_all x2, starting transfers between devices, scatter(): return lax.all_to_all(part, ('y', 'x'), 0, 0)  8.8 us
  transfers between devices with their start and end apart: 24, of which 14 were waited for; matrix products, arithmetic and copies ran while one was open for 3% of the time, Pallas kernels for 13%

profile of v3, /device:TPU:0, one launch (start us, length us, event | category | flops | bytes accessed | tf_op | source)
XLA Modules:
  0.0 175.7 jit_solution(1776664062714730820)
XLA Ops:
  1.9 2.7 %convolution_bitcast_fusion.2 = f32[1187,256]{1,0:T(8,128)S(1)} fusion(bf16[256,1024]{1,0:T(8,128)(2,1)S(1)} %bitcast.62, bf16[1024,1187]{0,1:T(8,128)(2,1)} %param.6), kind=kOutput, calls=%fused_computation.2 | convolution fusion | flops 622329856 | bytes 4170752 | tf_op jit(solution)/shard_map/dot_general | solution.py:51
  9.4 1.6 shard_map.76
  11.0 5.5 %collective-permute-start.4 = (s16[2,1200,128]{2,1,0:T(8,128)(2,1)}, s16[2,1200,128]{2,1,0:T(8,128)(2,1)S(1)}, u32[]{:S(2)}, u32[]{:S(2)}) collective-permute-start(s16[2,1200,128]{2,1,0:T(8,128)(2,1)} %shard_map.76), channel_id=1, source_target_pairs={{0,128},{128,0},{1,129},{129,1},{2,130},{130,2},{3,131},{131,3},{4... | collective-permute-start | bytes 1843208 | tf_op jit(solution)/shard_map/ppermute | solution.py:36
  25.2 1.9 %copy-done.5 = bf16[1280,1187]{0,1:T(8,128)(2,1)S(1)} copy-done((bf16[1280,1187]{0,1:T(8,128)(2,1)S(1)}, bf16[1280,1187]{0,1:T(8,128)(2,1)}, u32[]{:S(2)}) %copy-start.5) | copy-done | bytes 3038744
  27.1 5.9 %shard_map.78 = (f32[1187,256]{1,0:T(8,128)S(1)}, f32[1187,256]{1,0:T(8,128)S(1)}, f32[1187,256]{1,0:T(8,128)S(1)}, f32[1187,256]{1,0:T(8,128)S(1)}) custom-call(s32[4]{0:T(128)S(1)} %pad_add_fusion.1._, bf16[1024,1280]{1,0:T(8,128)(2,1)S(1)} %copy-done, bf16[1024,1280]{1,0:T(8,128)(2,1)S(1)} %copy-done, bf16[1024,1280]{1,0:T(8,128)(2,1)S(1)} %copy-done, ...), custom_call_target="tpu_custom_call" | custom-call | flops 1 | bytes 1 | tf_op jit(solution)/shard_map/pallas_call | solution.py:81
  34.5 5.6 %collective-permute-start.11 = (s16[2,1200,128]{2,1,0:T(8,128)(2,1)S(1)}, s16[2,1200,128]{2,1,0:T(8,128)(2,1)S(1)}, u32[]{:S(2)}, u32[]{:S(2)}) collective-permute-start(s16[2,1200,128]{2,1,0:T(8,128)(2,1)S(1)} %shard_map.77), channel_id=1, source_target_pairs={{0,128},{128,0},{1,129},{129,1},{2,130},{130,2},{3,131},{131,3},{4... | collective-permute-start | bytes 1843208 | tf_op jit(solution)/shard_map/ppermute | solution.py:36
  40.2 1.5 shard_map.80
  41.6 23.5 %all_to_all.20.many = f32[16,8,128]{2,1,0:T(8,128)S(1)} all-to-all(f32[16,8,128]{2,1,0:T(8,128)S(1)} %get-tuple-element.28), channel_id=1, replica_groups=mesh['g'=2,'s'=2,'z'=4,'y'=4,'x'=4] {'y','x'}, dimensions={0} | all-to-all | bytes 131072 | tf_op jit(solution)/shard_map/all_to_all | solution.py:217
  65.2 3.1 %collective-permute-start.7 = (f32[8,128]{1,0:T(8,128)S(1)}, f32[8,128]{1,0:T(8,128)S(1)}, u32[]{:S(2)}, u32[]{:S(2)}) collective-permute-start(f32[8,128]{1,0:T(8,128)S(1)} %shard_map.81.s0), channel_id=1, source_target_pairs={{0,32},{16,48},{32,0},{48,16},{1,33},{17,49},{33,1},{49,17},{2,34}... | collective-permute-start | bytes 12296 | tf_op jit(solution)/shard_map/ppermute | solution.py:40
  69.2 5.5 %collective-permute-done.8.s3 = f32[8,128]{1,0:T(8,128)S(1)} collective-permute-done((f32[8,128]{1,0:T(8,128)S(1)}, f32[8,128]{1,0:T(8,128)S(1)}, u32[]{:S(2)}, u32[]{:S(2)}) %collective-permute-start.8) | collective-permute-done | bytes 4128 | tf_op jit(solution)/shard_map/ppermute | solution.py:40
  74.7 1.5 collective-permute-done.7.s2
  77.4 4.2 %collective-permute-start.10 = (bf16[1200,128]{1,0:T(8,128)(2,1)S(1)}, bf16[1200,128]{1,0:T(8,128)(2,1)S(1)}, u32[]{:S(2)}, u32[]{:S(2)}) collective-permute-start(bf16[1200,128]{1,0:T(8,128)(2,1)S(1)} %shard_map.82.refs_0_), channel_id=1, source_target_pairs={{0,128},{128,0},{1,129},{129,1},{2,130},{130,2},{3,131},{131,3},{4... | collective-permute-start | bytes 921608 | tf_op jit(solution)/shard_map/ppermute | solution.py:36
  81.5 1.5 shard_map.84
  83.0 14.3 %all_to_all.21.many = f32[16,8,128]{2,1,0:T(8,128)S(1)} all-to-all(f32[16,8,128]{2,1,0:T(8,128)S(1)} %get-tuple-element.33), channel_id=1, replica_groups=mesh['g'=2,'s'=2,'z'=4,'y'=4,'x'=4] {'y','x'}, dimensions={0} | all-to-all | bytes 131072 | tf_op jit(solution)/shard_map/all_to_all | solution.py:217
  97.4 2.0 %collective-permute-start.13 = (f32[8,128]{1,0:T(8,128)S(1)}, f32[8,128]{1,0:T(8,128)S(1)}, u32[]{:S(2)}, u32[]{:S(2)}) collective-permute-start(f32[8,128]{1,0:T(8,128)S(1)} %shard_map.85.s0), channel_id=1, source_target_pairs={{0,32},{16,48},{32,0},{48,16},{1,33},{17,49},{33,1},{49,17},{2,34}... | collective-permute-start | bytes 12296 | tf_op jit(solution)/shard_map/ppermute | solution.py:40
  99.4 1.6 collective-permute-done.14.s3
  102.0 2.8 %collective-permute-done.12.s1 = f32[8,128]{1,0:T(8,128)S(1)} collective-permute-done((f32[8,128]{1,0:T(8,128)S(1)}, f32[8,128]{1,0:T(8,128)S(1)}, u32[]{:S(2)}, u32[]{:S(2)}) %collective-permute-start.12) | collective-permute-done | bytes 4128 | tf_op jit(solution)/shard_map/ppermute | solution.py:40
  104.8 1.9 %shard_map.86.refs_0_.refs_4_ = bf16[1200,128]{1,0:T(8,128)(2,1)} custom-call(s32[3]{0:T(128)S(1)} %pad_add_fusion.place, f32[8,128]{1,0:T(8,128)S(1)} %shard_map.85.s0, f32[8,128]{1,0:T(8,128)S(1)} %collective-permute-done.12.s1, f32[8,128]{1,0:T(8,128)S(1)} %collective-permute-done.13.s2, f32[8,128]{1,0:T(8,128)S(1)} %collective-permute-done.14.s3, ...), custom_call_target="tpu_custom_call" | custom-call | flops 1 | bytes 1 | tf_op jit(solution)/shard_map/pallas_call | solution.py:261
  106.8 2.0 %collective-permute-start.17 = (bf16[1200,128]{1,0:T(8,128)(2,1)}, bf16[1200,128]{1,0:T(8,128)(2,1)}, u32[]{:S(2)}, u32[]{:S(2)}) collective-permute-start(bf16[1200,128]{1,0:T(8,128)(2,1)} %shard_map.86.refs_0_.refs_4_), channel_id=1, source_target_pairs={{0,128},{128,0},{1,129},{129,1},{2,130},{130,2},{3,131},{131,3},{4... | collective-permute-start | bytes 921608 | tf_op jit(solution)/shard_map/ppermute | solution.py:36
  108.8 2.5 %shard_map.87 = bf16[16,32,1280]{2,1,0:T(8,128)(2,1)S(1)} custom-call(s32[3]{0:T(128)S(1)} %pad_add_fusion.place, bf16[1200,128]{1,0:T(8,128)(2,1)S(1)} %shard_map.82.refs_0_, bf16[1200,128]{1,0:T(8,128)(2,1)S(1)} %collective-permute-done.9.refs_1_, bf16[1200,128]{1,0:T(8,128)(2,1)S(1)} %collective-permute-done.10.refs_2_, ...), custom_call_target="tpu_custom_call" | custom-call | flops 1 | bytes 1 | tf_op jit(solution)/shard_map/pallas_call | solution.py:286
  113.0 4.4 %all-to-all-start.2 = ((bf16[16,32,1280]{2,1,0:T(8,128)(2,1)}), bf16[16,32,1280]{2,1,0:T(8,128)(2,1)}, u32[]{:S(2)}, u32[]{:S(2)}) async-start(bf16[16,32,1280]{2,1,0:T(8,128)(2,1)} %copy-done.10), calls=%async_computation.2 | async-start | bytes 2621440 | tf_op jit(solution)/shard_map/all_to_all | solution.py:297
  117.7 7.9 %collective-permute-done.17.refs_2_.refs_6_ = bf16[1200,128]{1,0:T(8,128)(2,1)} collective-permute-done((bf16[1200,128]{1,0:T(8,128)(2,1)}, bf16[1200,128]{1,0:T(8,128)(2,1)}, u32[]{:S(2)}, u32[]{:S(2)}) %collective-permute-start.17) | collective-permute-done | bytes 307232 | tf_op jit(solution)/shard_map/ppermute | solution.py:36
  125.7 1.7 collective-permute-done.18.refs_3_.refs_7_
  127.5 1.9 %copy-done.7 = bf16[1280,1187]{0,1:T(8,128)(2,1)S(1)} copy-done((bf16[1280,1187]{0,1:T(8,128)(2,1)S(1)}, bf16[1280,1187]{0,1:T(8,128)(2,1)}, u32[]{:S(2)}) %copy-start.7) | copy-done | bytes 3038744
  129.3 3.0 %shard_map.88 = bf16[16,32,1280]{2,1,0:T(8,128)(2,1)S(1)} custom-call(s32[3]{0:T(128)S(1)} %pad_add_fusion.place, bf16[1200,128]{1,0:T(8,128)(2,1)} %shard_map.86.refs_0_.refs_4_, bf16[1200,128]{1,0:T(8,128)(2,1)S(1)} %collective-permute-done.16.refs_1_.refs_5_, bf16[1200,128]{1,0:T(8,128)(2,1)} %collective-permute-done.17.refs_2_.refs_6_, ...), custom_call_target="tpu_custom_call" | custom-call | flops 8200000000 | bytes 1 | tf_op jit(solution)/shard_map/pallas_call | solution.py:286
  134.9 5.1 %all-to-all-done.2 = bf16[16,32,1280]{2,1,0:T(8,128)(2,1)} async-done(((bf16[16,32,1280]{2,1,0:T(8,128)(2,1)}), bf16[16,32,1280]{2,1,0:T(8,128)(2,1)}, u32[]{:S(2)}, u32[]{:S(2)}) %all-to-all-start.2) | async-done | bytes 1310752 | tf_op jit(solution)/shard_map/all_to_all | solution.py:297
  140.0 4.4 %all-to-all-start.3 = ((bf16[16,32,1280]{2,1,0:T(8,128)(2,1)}), bf16[16,32,1280]{2,1,0:T(8,128)(2,1)}, u32[]{:S(2)}, u32[]{:S(2)}) async-start(bf16[16,32,1280]{2,1,0:T(8,128)(2,1)} %copy-done.17), calls=%async_computation.3 | async-start | bytes 2621440 | tf_op jit(solution)/shard_map/all_to_all | solution.py:297
  147.5 6.8 %shard_map.89 = (bf16[1187,1280]{1,0:T(8,128)(2,1)}, f32[8,128]{1,0:T(8,128)S(1)}) custom-call(s32[8]{0:T(128)S(1)} %stack.59._, bf16[1200,128]{1,0:T(8,128)(2,1)S(1)} %shard_map.82.refs_0_, bf16[1200,128]{1,0:T(8,128)(2,1)S(1)} %collective-permute-done.9.refs_1_, bf16[1200,128]{1,0:T(8,128)(2,1)S(1)} %collective-permute-done.10.refs_2_, ...), custom_call_target="tpu_custom_call" | custom-call | flops 3111649280 | bytes 6077440 | tf_op jit(solution)/shard_map/pallas_call | solution.py:333
  154.3 1.5 convert_reduce_fusion.1
  155.8 9.2 %all-to-all-done.3 = bf16[16,32,1280]{2,1,0:T(8,128)(2,1)} async-done(((bf16[16,32,1280]{2,1,0:T(8,128)(2,1)}), bf16[16,32,1280]{2,1,0:T(8,128)(2,1)}, u32[]{:S(2)}, u32[]{:S(2)}) %all-to-all-start.3) | async-done | bytes 1310752 | tf_op jit(solution)/shard_map/all_to_all | solution.py:297
  165.0 1.5 convert_reduce_fusion
  167.9 2.6 %collective-permute-start.21 = (f32[16,1280]{1,0:T(8,128)S(1)}, f32[16,1280]{1,0:T(8,128)S(1)}, u32[]{:S(2)}, u32[]{:S(2)}) collective-permute-start(f32[16,1280]{1,0:T(8,128)S(1)} %get-tuple-element.49), channel_id=1, source_target_pairs={{0,48},{16,0},{32,16},{48,32},{1,49},{17,1},{33,17},{49,33},{2,50}... | collective-permute-start | bytes 245768 | tf_op jit(solution)/shard_map/ppermute | solution.py:40
  (98 shorter events, 31.9 us)
Async XLA Ops:
  1.9 2.8 %copy-start = (bf16[1024,1280]{1,0:T(8,128)(2,1)S(1)}, bf16[1024,1280]{1,0:T(8,128)(2,1)}, u32[]{:S(2)}) copy-start(bf16[1024,1280]{1,0:T(8,128)(2,1)} %refs_15_.1) | copy-start | bytes 7864324
  1.9 3.4 %copy-start.4 = (bf16[1280,1187]{0,1:T(8,128)(2,1)S(1)}, bf16[1280,1187]{0,1:T(8,128)(2,1)}, u32[]{:S(2)}) copy-start(bf16[1280,1187]{0,1:T(8,128)(2,1)} %param.8) | copy-start | bytes 9116164
  4.6 4.3 %collective-permute-start.1 = (f32[1187,256]{1,0:T(8,128)S(1)}, f32[1187,256]{1,0:T(8,128)S(1)}, u32[]{:S(2)}, u32[]{:S(2)}) collective-permute-start(f32[1187,256]{1,0:T(8,128)S(1)} %convolution_bitcast_fusion.2), channel_id=1, source_target_pairs={{0,64},{64,0},{1,65},{65,1},{2,66},{66,2},{3,67},{67,3},{4,68},{68... | collective-permute-start | bytes 3646472 | tf_op jit(solution)/shard_map/ppermute | solution.py:36
  6.3 3.1 %collective-permute-start = (f32[1187,256]{1,0:T(8,128)S(1)}, f32[1187,256]{1,0:T(8,128)S(1)}, u32[]{:S(2)}, u32[]{:S(2)}) collective-permute-start(f32[1187,256]{1,0:T(8,128)S(1)} %convolution_bitcast_fusion), channel_id=1, source_target_pairs={{0,64},{64,0},{1,65},{65,1},{2,66},{66,2},{3,67},{67,3},{4,68},{68... | collective-permute-start | bytes 3646472 | tf_op jit(solution)/shard_map/ppermute | solution.py:36
  8.9 2.0 %copy-start.15 = (f32[1187,256]{1,0:T(8,128)}, f32[1187,256]{1,0:T(8,128)S(1)}, u32[]{:S(2)}) copy-start(f32[1187,256]{1,0:T(8,128)S(1)} %convolution_bitcast_fusion.1.as_) | copy-start | bytes 3646468
  9.0 7.6 %copy-start.24 = (s32[256]{0:T(256)S(1)}, s32[256]{0:T(256)}, u32[]{:S(2)}) copy-start(s32[256]{0:T(256)} %param.9) | copy-start | bytes 3076
  9.0 2.0 %copy-start.11 = (f32[1187,256]{1,0:T(8,128)}, f32[1187,256]{1,0:T(8,128)S(1)}, u32[]{:S(2)}) copy-start(f32[1187,256]{1,0:T(8,128)S(1)} %collective-permute-done.1.bt) | copy-start | bytes 3646468
  11.0 23.5 %collective-permute-start.4 = (s16[2,1200,128]{2,1,0:T(8,128)(2,1)}, s16[2,1200,128]{2,1,0:T(8,128)(2,1)S(1)}, u32[]{:S(2)}, u32[]{:S(2)}) collective-permute-start(s16[2,1200,128]{2,1,0:T(8,128)(2,1)} %shard_map.76), channel_id=1, source_target_pairs={{0,128},{128,0},{1,129},{129,1},{2,130},{130,2},{3,131},{131,3},{4... | collective-permute-start | bytes 1843208 | tf_op jit(solution)/shard_map/ppermute | solution.py:36
  16.5 1.2 collective-permute-start.5
  22.9 2.3 %copy-start.3 = (bf16[1024,1187]{0,1:T(8,128)(2,1)S(1)}, bf16[1024,1187]{0,1:T(8,128)(2,1)}, u32[]{:S(2)}) copy-start(bf16[1024,1187]{0,1:T(8,128)(2,1)} %param.6) | copy-start | bytes 7292932
  33.0 7.2 %collective-permute-start.2 = (f32[1187,256]{1,0:T(8,128)S(1)}, f32[1187,256]{1,0:T(8,128)S(1)}, u32[]{:S(2)}, u32[]{:S(2)}) collective-permute-start(f32[1187,256]{1,0:T(8,128)S(1)} %get-tuple-element.25), channel_id=1, source_target_pairs={{0,64},{64,0},{1,65},{65,1},{2,66},{66,2},{3,67},{67,3},{4,68},{68... | collective-permute-start | bytes 3646472 | tf_op jit(solution)/shard_map/ppermute | solution.py:36
  33.3 6.9 %collective-permute-start.3 = (f32[1187,256]{1,0:T(8,128)S(1)}, f32[1187,256]{1,0:T(8,128)S(1)}, u32[]{:S(2)}, u32[]{:S(2)}) collective-permute-start(f32[1187,256]{1,0:T(8,128)S(1)} %get-tuple-element.27), channel_id=1, source_target_pairs={{0,64},{64,0},{1,65},{65,1},{2,66},{66,2},{3,67},{67,3},{4,68},{68... | collective-permute-start | bytes 3646472 | tf_op jit(solution)/shard_map/ppermute | solution.py:36
  34.5 34.7 %collective-permute-start.11 = (s16[2,1200,128]{2,1,0:T(8,128)(2,1)S(1)}, s16[2,1200,128]{2,1,0:T(8,128)(2,1)S(1)}, u32[]{:S(2)}, u32[]{:S(2)}) collective-permute-start(s16[2,1200,128]{2,1,0:T(8,128)(2,1)S(1)} %shard_map.77), channel_id=1, source_target_pairs={{0,128},{128,0},{1,129},{129,1},{2,130},{130,2},{3,131},{131,3},{4... | collective-permute-start | bytes 1843208 | tf_op jit(solution)/shard_map/ppermute | solution.py:36
  65.1 9.5 %collective-permute-start.8 = (f32[8,128]{1,0:T(8,128)S(1)}, f32[8,128]{1,0:T(8,128)S(1)}, u32[]{:S(2)}, u32[]{:S(2)}) collective-permute-start(f32[8,128]{1,0:T(8,128)S(1)} %shard_map.81.s0), channel_id=1, source_target_pairs={{0,48},{16,0},{32,16},{48,32},{1,49},{17,1},{33,17},{49,33},{2,50}... | collective-permute-start | bytes 12296 | tf_op jit(solution)/shard_map/ppermute | solution.py:40
  65.2 10.9 %collective-permute-start.7 = (f32[8,128]{1,0:T(8,128)S(1)}, f32[8,128]{1,0:T(8,128)S(1)}, u32[]{:S(2)}, u32[]{:S(2)}) collective-permute-start(f32[8,128]{1,0:T(8,128)S(1)} %shard_map.81.s0), channel_id=1, source_target_pairs={{0,32},{16,48},{32,0},{48,16},{1,33},{17,49},{33,1},{49,17},{2,34}... | collective-permute-start | bytes 12296 | tf_op jit(solution)/shard_map/ppermute | solution.py:40
  68.3 7.9 %collective-permute-start.6 = (f32[8,128]{1,0:T(8,128)S(1)}, f32[8,128]{1,0:T(8,128)S(1)}, u32[]{:S(2)}, u32[]{:S(2)}) collective-permute-start(f32[8,128]{1,0:T(8,128)S(1)} %shard_map.81.s0), channel_id=1, source_target_pairs={{0,16},{16,32},{32,48},{48,0},{1,17},{17,33},{33,49},{49,1},{2,18}... | collective-permute-start | bytes 12296 | tf_op jit(solution)/shard_map/ppermute | solution.py:40
  77.4 29.4 %collective-permute-start.10 = (bf16[1200,128]{1,0:T(8,128)(2,1)S(1)}, bf16[1200,128]{1,0:T(8,128)(2,1)S(1)}, u32[]{:S(2)}, u32[]{:S(2)}) collective-permute-start(bf16[1200,128]{1,0:T(8,128)(2,1)S(1)} %shard_map.82.refs_0_), channel_id=1, source_target_pairs={{0,128},{128,0},{1,129},{129,1},{2,130},{130,2},{3,131},{131,3},{4... | collective-permute-start | bytes 921608 | tf_op jit(solution)/shard_map/ppermute | solution.py:36
  81.5 27.2 %copy-start.6 = (bf16[1280,1187]{0,1:T(8,128)(2,1)S(1)}, bf16[1280,1187]{0,1:T(8,128)(2,1)}, u32[]{:S(2)}) copy-start(bf16[1280,1187]{0,1:T(8,128)(2,1)} %param.8) | copy-start | bytes 9116164
  97.3 3.7 %collective-permute-start.14 = (f32[8,128]{1,0:T(8,128)S(1)}, f32[8,128]{1,0:T(8,128)S(1)}, u32[]{:S(2)}, u32[]{:S(2)}) collective-permute-start(f32[8,128]{1,0:T(8,128)S(1)} %shard_map.85.s0), channel_id=1, source_target_pairs={{0,48},{16,0},{32,16},{48,32},{1,49},{17,1},{33,17},{49,33},{2,50}... | collective-permute-start | bytes 12296 | tf_op jit(solution)/shard_map/ppermute | solution.py:40
  97.4 4.6 %collective-permute-start.13 = (f32[8,128]{1,0:T(8,128)S(1)}, f32[8,128]{1,0:T(8,128)S(1)}, u32[]{:S(2)}, u32[]{:S(2)}) collective-permute-start(f32[8,128]{1,0:T(8,128)S(1)} %shard_map.85.s0), channel_id=1, source_target_pairs={{0,32},{16,48},{32,0},{48,16},{1,33},{17,49},{33,1},{49,17},{2,34}... | collective-permute-start | bytes 12296 | tf_op jit(solution)/shard_map/ppermute | solution.py:40
  99.4 5.4 %collective-permute-start.12 = (f32[8,128]{1,0:T(8,128)S(1)}, f32[8,128]{1,0:T(8,128)S(1)}, u32[]{:S(2)}, u32[]{:S(2)}) collective-permute-start(f32[8,128]{1,0:T(8,128)S(1)} %shard_map.85.s0), channel_id=1, source_target_pairs={{0,16},{16,32},{32,48},{48,0},{1,17},{17,33},{33,49},{49,1},{2,18}... | collective-permute-start | bytes 12296 | tf_op jit(solution)/shard_map/ppermute | solution.py:40
  99.4 9.3 %collective-permute-start.9 = (bf16[1200,128]{1,0:T(8,128)(2,1)S(1)}, bf16[1200,128]{1,0:T(8,128)(2,1)S(1)}, u32[]{:S(2)}, u32[]{:S(2)}) collective-permute-start(bf16[1200,128]{1,0:T(8,128)(2,1)S(1)} %shard_map.82.refs_0_), channel_id=1, source_target_pairs={{0,64},{64,0},{1,65},{65,1},{2,66},{66,2},{3,67},{67,3},{4,68},{68... | collective-permute-start | bytes 921608 | tf_op jit(solution)/shard_map/ppermute | solution.py:36
  106.8 2.0 %collective-permute-start.15 = (bf16[1200,128]{1,0:T(8,128)(2,1)S(1)}, bf16[1200,128]{1,0:T(8,128)(2,1)S(1)}, u32[]{:S(2)}, u32[]{:S(2)}) collective-permute-start(bf16[1200,128]{1,0:T(8,128)(2,1)S(1)} %collective-permute-done.10.refs_2_), channel_id=1, source_target_pairs={{0,64},{64,0},{1,65},{65,1},{2,66},{66,2},{3,67},{67,3},{4,68},{68... | collective-permute-start | bytes 921608 | tf_op jit(solution)/shard_map/ppermute | solution.py:36
  106.8 18.9 %collective-permute-start.17 = (bf16[1200,128]{1,0:T(8,128)(2,1)}, bf16[1200,128]{1,0:T(8,128)(2,1)}, u32[]{:S(2)}, u32[]{:S(2)}) collective-permute-start(bf16[1200,128]{1,0:T(8,128)(2,1)} %shard_map.86.refs_0_.refs_4_), channel_id=1, source_target_pairs={{0,128},{128,0},{1,129},{129,1},{2,130},{130,2},{3,131},{131,3},{4... | collective-permute-start | bytes 921608 | tf_op jit(solution)/shard_map/ppermute | solution.py:36
  113.0 26.9 %all-to-all-start.2 = ((bf16[16,32,1280]{2,1,0:T(8,128)(2,1)}), bf16[16,32,1280]{2,1,0:T(8,128)(2,1)}, u32[]{:S(2)}, u32[]{:S(2)}) async-start(bf16[16,32,1280]{2,1,0:T(8,128)(2,1)} %copy-done.10), calls=%async_computation.2 | async-start | bytes 2621440 | tf_op jit(solution)/shard_map/all_to_all | solution.py:297
  117.4 8.3 %collective-permute-start.16 = (bf16[1200,128]{1,0:T(8,128)(2,1)}, bf16[1200,128]{1,0:T(8,128)(2,1)S(1)}, u32[]{:S(2)}, u32[]{:S(2)}) collective-permute-start(bf16[1200,128]{1,0:T(8,128)(2,1)} %shard_map.86.refs_0_.refs_4_), channel_id=1, source_target_pairs={{0,64},{64,0},{1,65},{65,1},{2,66},{66,2},{3,67},{67,3},{4,68},{68... | collective-permute-start | bytes 921608 | tf_op jit(solution)/shard_map/ppermute | solution.py:36
  125.7 1.8 %collective-permute-start.18 = (bf16[1200,128]{1,0:T(8,128)(2,1)}, bf16[1200,128]{1,0:T(8,128)(2,1)S(1)}, u32[]{:S(2)}, u32[]{:S(2)}) collective-permute-start(bf16[1200,128]{1,0:T(8,128)(2,1)} %collective-permute-done.17.refs_2_.refs_6_), channel_id=1, source_target_pairs={{0,64},{64,0},{1,65},{65,1},{2,66},{66,2},{3,67},{67,3},{4,68},{68... | collective-permute-start | bytes 921608 | tf_op jit(solution)/shard_map/ppermute | solution.py:36
  127.5 1.9 %copy-start.7 = (bf16[1280,1187]{0,1:T(8,128)(2,1)S(1)}, bf16[1280,1187]{0,1:T(8,128)(2,1)}, u32[]{:S(2)}) copy-start(bf16[1280,1187]{0,1:T(8,128)(2,1)} %param.8) | copy-start | bytes 9116164
  140.0 25.1 %all-to-all-start.3 = ((bf16[16,32,1280]{2,1,0:T(8,128)(2,1)}), bf16[16,32,1280]{2,1,0:T(8,128)(2,1)}, u32[]{:S(2)}, u32[]{:S(2)}) async-start(bf16[16,32,1280]{2,1,0:T(8,128)(2,1)} %copy-done.17), calls=%async_computation.3 | async-start | bytes 2621440 | tf_op jit(solution)/shard_map/all_to_all | solution.py:297
  166.6 6.4 %collective-permute-start.19 = (f32[16,1280]{1,0:T(8,128)S(1)}, f32[16,1280]{1,0:T(8,128)S(1)}, u32[]{:S(2)}, u32[]{:S(2)}) collective-permute-start(f32[16,1280]{1,0:T(8,128)S(1)} %get-tuple-element.47), channel_id=1, source_target_pairs={{0,16},{16,32},{32,48},{48,0},{1,17},{17,33},{33,49},{49,1},{2,18}... | collective-permute-start | bytes 245768 | tf_op jit(solution)/shard_map/ppermute | solution.py:40
  166.7 6.3 %collective-permute-start.20 = (f32[16,1280]{1,0:T(8,128)S(1)}, f32[16,1280]{1,0:T(8,128)S(1)}, u32[]{:S(2)}, u32[]{:S(2)}) collective-permute-start(f32[16,1280]{1,0:T(8,128)S(1)} %get-tuple-element.48), channel_id=1, source_target_pairs={{0,32},{16,48},{32,0},{48,16},{1,33},{17,49},{33,1},{49,17},{2,34}... | collective-permute-start | bytes 245768 | tf_op jit(solution)/shard_map/ppermute | solution.py:40
  167.9 6.0 %collective-permute-start.21 = (f32[16,1280]{1,0:T(8,128)S(1)}, f32[16,1280]{1,0:T(8,128)S(1)}, u32[]{:S(2)}, u32[]{:S(2)}) collective-permute-start(f32[16,1280]{1,0:T(8,128)S(1)} %get-tuple-element.49), channel_id=1, source_target_pairs={{0,48},{16,0},{32,16},{48,32},{1,49},{17,1},{33,17},{49,33},{2,50}... | collective-permute-start | bytes 245768 | tf_op jit(solution)/shard_map/ppermute | solution.py:40
  (17 other events, 20.6 us)

commit v4 on v3

--- a/solution.py
+++ b/solution.py
@@ -282,13 +282,17 @@
 
 
 def hidden_part(place, pairs, w, flops):
-    depth, n = w.shape[1], len(pairs)
+    (width, depth), n = w.shape, len(pairs)
+    tile = depth // 2
     return pl.pallas_call(
         hidden_kernel,
-        in_specs=[SMEM] + [VMEM] * (2 * n + 1),
-        out_specs=VMEM,
+        grid=(2,),
+        in_specs=[SMEM]
+        + [pl.BlockSpec(v.shape, lambda i: (0, 0)) for pair in pairs for v in pair]
+        + [pl.BlockSpec((width, tile), lambda i: (0, i))],
+        out_specs=pl.BlockSpec((16, 16 * n, tile), lambda i: (0, 0, i)),
         out_shape=jax.ShapeDtypeStruct((16, 16 * n, depth), BF16),
-        compiler_params=params(24),
+        compiler_params=params(60),
         cost_estimate=estimate(flops),
     )(place, *[v for pair in pairs for v in pair], w)
 

time: 178 us -> 180 us (1.011)
  Pallas kernels: 26.4 us -> 31.1 us
  local copies, waits for them, and re-layouts: 20.3 us -> 16.4 us
    pallas_call x2, Pallas kernels: 5.5 us -> 10.2 us  [hidden_part(): pl.pallas_call(hidden_kernel, grid=(2,), in_specs=[SMEM] + [pl.BlockSpec(...]
    unnamed x50 -> x56, local copies, waits for them, and re-layouts: 18.9 us -> 14.9 us
    all_to_all x2, waiting for transfers between devices: 14.2 us -> 17.5 us  [scatter(): return lax.all_to_all(part, ('y', 'x'), 0, 0)]
    ppermute x13, waiting for transfers between devices: 12 us -> 9.79 us  [swap(): return lax.ppermute(x, axis, [(0, 1), (1, 0)])]
  transfers between devices with their start and end apart: 24 -> 24, of which waited for: 14 -> 14; matrix products, arithmetic and copies ran while one was open for 3% -> 3% of each run, Pallas kernels for 13% -> 16%
where the time goes in v4:
time: 180 us; the launch traced here: 178 us
  waiting for transfers between devices  41.8 us (23%)
  blocking collectives  37.8 us (21%)
  starting transfers between devices  37.5 us (21%)
  Pallas kernels  31.1 us (17%)
  local copies, waits for them, and re-layouts  16.4 us (9%)
  matrix products  5.61 us (3%)
  other arithmetic  4.48 us (2%)
  between operations  2.91 us (2%)
    all_to_all x2, blocking collectives, all_stats(): many = lax.all_to_all(stats, ('y', 'x'), 0, 0)  37.8 us
    ppermute x13, starting transfers between devices, swap(): return lax.ppermute(x, axis, [(0, 1), (1, 0)])  18.6 us
    all_to_all x2, waiting for transfers between devices, scatter(): return lax.all_to_all(part, ('y', 'x'), 0, 0)  17.5 us
    unnamed x56, local copies, waits for them, and re-layouts  14.9 us
    ppermute x9, waiting for transfers between devices, rotate(): return lax.ppermute(x, axis, [(i, (i + step) % size) for i in range(size)])  14.5 us
    pallas_call x2, Pallas kernels, hidden_part(): pl.pallas_call(hidden_kernel, grid=(2,), in_specs=[SMEM] + [pl.BlockSpec(...  10.2 us
    ppermute x9, starting transfers between devices, rotate(): return lax.ppermute(x, axis, [(i, (i + step) % size) for i in range(size)])  9.88 us
    ppermute x13, waiting for transfers between devices, swap(): return lax.ppermute(x, axis, [(0, 1), (1, 0)])  9.79 us
  transfers between devices with their start and end apart: 24, of which 14 were waited for; matrix products, arithmetic and copies ran while one was open for 3% of the time, Pallas kernels for 16%

profile of v4, /device:TPU:0, one launch (start us, length us, event | category | flops | bytes accessed | tf_op | source)
XLA Modules:
  0.0 177.6 jit_solution(12052001409165865849)
XLA Ops:
  0.6 1.3 constant_dynamic-slice_fusion.2
  1.9 2.7 %convolution_bitcast_fusion.2 = f32[1187,256]{1,0:T(8,128)S(1)} fusion(bf16[256,1024]{1,0:T(8,128)(2,1)S(1)} %bitcast.62, bf16[1024,1187]{0,1:T(8,128)(2,1)} %param.6), kind=kOutput, calls=%fused_computation.2 | convolution fusion | flops 622329856 | bytes 4170752 | tf_op jit(solution)/shard_map/dot_general | solution.py:51
  9.4 1.6 shard_map.76
  11.0 5.5 %collective-permute-start.4 = (s16[2,1200,128]{2,1,0:T(8,128)(2,1)}, s16[2,1200,128]{2,1,0:T(8,128)(2,1)S(1)}, u32[]{:S(2)}, u32[]{:S(2)}) collective-permute-start(s16[2,1200,128]{2,1,0:T(8,128)(2,1)} %shard_map.76), channel_id=1, source_target_pairs={{0,128},{128,0},{1,129},{129,1},{2,130},{130,2},{3,131},{131,3},{4... | collective-permute-start | bytes 1843208 | tf_op jit(solution)/shard_map/ppermute | solution.py:36
  25.2 1.9 %copy-done.5 = bf16[1280,1187]{0,1:T(8,128)(2,1)S(1)} copy-done((bf16[1280,1187]{0,1:T(8,128)(2,1)S(1)}, bf16[1280,1187]{0,1:T(8,128)(2,1)}, u32[]{:S(2)}) %copy-start.5) | copy-done | bytes 3038744
  27.1 5.9 %shard_map.78 = (f32[1187,256]{1,0:T(8,128)S(1)}, f32[1187,256]{1,0:T(8,128)S(1)}, f32[1187,256]{1,0:T(8,128)S(1)}, f32[1187,256]{1,0:T(8,128)S(1)}) custom-call(s32[4]{0:T(128)S(1)} %pad_add_fusion.1._, bf16[1024,1280]{1,0:T(8,128)(2,1)S(1)} %copy-done, bf16[1024,1280]{1,0:T(8,128)(2,1)S(1)} %copy-done, bf16[1024,1280]{1,0:T(8,128)(2,1)S(1)} %copy-done, ...), custom_call_target="tpu_custom_call" | custom-call | flops 1 | bytes 1 | tf_op jit(solution)/shard_map/pallas_call | solution.py:81
  34.6 5.6 %collective-permute-start.11 = (s16[2,1200,128]{2,1,0:T(8,128)(2,1)S(1)}, s16[2,1200,128]{2,1,0:T(8,128)(2,1)S(1)}, u32[]{:S(2)}, u32[]{:S(2)}) collective-permute-start(s16[2,1200,128]{2,1,0:T(8,128)(2,1)S(1)} %shard_map.77), channel_id=1, source_target_pairs={{0,128},{128,0},{1,129},{129,1},{2,130},{130,2},{3,131},{131,3},{4... | collective-permute-start | bytes 1843208 | tf_op jit(solution)/shard_map/ppermute | solution.py:36
  40.2 1.5 shard_map.80
  41.7 23.5 %all_to_all.20.many = f32[16,8,128]{2,1,0:T(8,128)S(1)} all-to-all(f32[16,8,128]{2,1,0:T(8,128)S(1)} %get-tuple-element.28), channel_id=1, replica_groups=mesh['g'=2,'s'=2,'z'=4,'y'=4,'x'=4] {'y','x'}, dimensions={0} | all-to-all | bytes 131072 | tf_op jit(solution)/shard_map/all_to_all | solution.py:217
  65.3 3.0 %collective-permute-start.7 = (f32[8,128]{1,0:T(8,128)S(1)}, f32[8,128]{1,0:T(8,128)S(1)}, u32[]{:S(2)}, u32[]{:S(2)}) collective-permute-start(f32[8,128]{1,0:T(8,128)S(1)} %shard_map.81.s0), channel_id=1, source_target_pairs={{0,32},{16,48},{32,0},{48,16},{1,33},{17,49},{33,1},{49,17},{2,34}... | collective-permute-start | bytes 12296 | tf_op jit(solution)/shard_map/ppermute | solution.py:40
  69.1 5.6 %collective-permute-done.8.s3 = f32[8,128]{1,0:T(8,128)S(1)} collective-permute-done((f32[8,128]{1,0:T(8,128)S(1)}, f32[8,128]{1,0:T(8,128)S(1)}, u32[]{:S(2)}, u32[]{:S(2)}) %collective-permute-start.8) | collective-permute-done | bytes 4128 | tf_op jit(solution)/shard_map/ppermute | solution.py:40
  74.7 1.5 collective-permute-done.7.s2
  77.4 4.2 %collective-permute-start.10 = (bf16[1200,128]{1,0:T(8,128)(2,1)S(1)}, bf16[1200,128]{1,0:T(8,128)(2,1)S(1)}, u32[]{:S(2)}, u32[]{:S(2)}) collective-permute-start(bf16[1200,128]{1,0:T(8,128)(2,1)S(1)} %shard_map.82.refs_0_), channel_id=1, source_target_pairs={{0,128},{128,0},{1,129},{129,1},{2,130},{130,2},{3,131},{131,3},{4... | collective-permute-start | bytes 921608 | tf_op jit(solution)/shard_map/ppermute | solution.py:36
  81.6 1.4 shard_map.84
  83.0 14.3 %all_to_all.21.many = f32[16,8,128]{2,1,0:T(8,128)S(1)} all-to-all(f32[16,8,128]{2,1,0:T(8,128)S(1)} %get-tuple-element.33), channel_id=1, replica_groups=mesh['g'=2,'s'=2,'z'=4,'y'=4,'x'=4] {'y','x'}, dimensions={0} | all-to-all | bytes 131072 | tf_op jit(solution)/shard_map/all_to_all | solution.py:217
  97.4 2.0 %collective-permute-start.13 = (f32[8,128]{1,0:T(8,128)S(1)}, f32[8,128]{1,0:T(8,128)S(1)}, u32[]{:S(2)}, u32[]{:S(2)}) collective-permute-start(f32[8,128]{1,0:T(8,128)S(1)} %shard_map.85.s0), channel_id=1, source_target_pairs={{0,32},{16,48},{32,0},{48,16},{1,33},{17,49},{33,1},{49,17},{2,34}... | collective-permute-start | bytes 12296 | tf_op jit(solution)/shard_map/ppermute | solution.py:40
  99.4 1.6 collective-permute-done.14.s3
  102.0 2.8 %collective-permute-done.12.s1 = f32[8,128]{1,0:T(8,128)S(1)} collective-permute-done((f32[8,128]{1,0:T(8,128)S(1)}, f32[8,128]{1,0:T(8,128)S(1)}, u32[]{:S(2)}, u32[]{:S(2)}) %collective-permute-start.12) | collective-permute-done | bytes 4128 | tf_op jit(solution)/shard_map/ppermute | solution.py:40
  104.8 1.9 %shard_map.86.refs_0_.refs_4_ = bf16[1200,128]{1,0:T(8,128)(2,1)} custom-call(s32[3]{0:T(128)S(1)} %pad_add_fusion.place, f32[8,128]{1,0:T(8,128)S(1)} %shard_map.85.s0, f32[8,128]{1,0:T(8,128)S(1)} %collective-permute-done.12.s1, f32[8,128]{1,0:T(8,128)S(1)} %collective-permute-done.13.s2, f32[8,128]{1,0:T(8,128)S(1)} %collective-permute-done.14.s3, ...), custom_call_target="tpu_custom_call" | custom-call | flops 1 | bytes 1 | tf_op jit(solution)/shard_map/pallas_call | solution.py:261
  106.8 2.1 %collective-permute-start.17 = (bf16[1200,128]{1,0:T(8,128)(2,1)}, bf16[1200,128]{1,0:T(8,128)(2,1)}, u32[]{:S(2)}, u32[]{:S(2)}) collective-permute-start(bf16[1200,128]{1,0:T(8,128)(2,1)} %shard_map.86.refs_0_.refs_4_), channel_id=1, source_target_pairs={{0,128},{128,0},{1,129},{129,1},{2,130},{130,2},{3,131},{131,3},{4... | collective-permute-start | bytes 921608 | tf_op jit(solution)/shard_map/ppermute | solution.py:36
  110.3 5.0 %shard_map.87 = bf16[16,32,1280]{2,1,0:T(8,128)(2,1)} custom-call(s32[3]{0:T(128)} %copy-done.26, bf16[1200,128]{1,0:T(8,128)(2,1)} %copy-done.14, bf16[1200,128]{1,0:T(8,128)(2,1)} %copy-done.18, bf16[1200,128]{1,0:T(8,128)(2,1)} %copy-done.16, bf16[1200,128]{1,0:T(8,128)(2,1)} %copy-done.20, bf16[1187,1280]{1,0:T(8,128)(2,1)} %bitcast.58), custom_call_target="tpu_custom_call" | custom-call | flops 1 | bytes 1 | tf_op jit(solution)/shard_map/pallas_call | solution.py:287
  115.3 4.4 %all-to-all-start.2 = ((bf16[16,32,1280]{2,1,0:T(8,128)(2,1)}), bf16[16,32,1280]{2,1,0:T(8,128)(2,1)}, u32[]{:S(2)}, u32[]{:S(2)}) async-start(bf16[16,32,1280]{2,1,0:T(8,128)(2,1)} %shard_map.87), calls=%async_computation.2 | async-start | bytes 2621440 | tf_op jit(solution)/shard_map/all_to_all | solution.py:301
  119.9 5.7 %collective-permute-done.17.refs_2_.refs_6_ = bf16[1200,128]{1,0:T(8,128)(2,1)} collective-permute-done((bf16[1200,128]{1,0:T(8,128)(2,1)}, bf16[1200,128]{1,0:T(8,128)(2,1)}, u32[]{:S(2)}, u32[]{:S(2)}) %collective-permute-start.17) | collective-permute-done | bytes 307232 | tf_op jit(solution)/shard_map/ppermute | solution.py:36
  125.7 1.7 collective-permute-done.18.refs_3_.refs_7_
  128.2 5.1 %shard_map.88 = bf16[16,32,1280]{2,1,0:T(8,128)(2,1)} custom-call(s32[3]{0:T(128)} %copy-done.26, bf16[1200,128]{1,0:T(8,128)(2,1)} %shard_map.86.refs_0_.refs_4_, bf16[1200,128]{1,0:T(8,128)(2,1)} %copy-done.22, bf16[1200,128]{1,0:T(8,128)(2,1)} %collective-permute-done.17.refs_2_.refs_6_, bf16[1200,128]{1,0:T(8,128)(2,1)} %copy-done.24, ...), custom_call_target="tpu_custom_call" | custom-call | flops 8200000000 | bytes 1 | tf_op jit(solution)/shard_map/pallas_call | solution.py:287
  133.3 8.6 %all-to-all-done.2 = bf16[16,32,1280]{2,1,0:T(8,128)(2,1)} async-done(((bf16[16,32,1280]{2,1,0:T(8,128)(2,1)}), bf16[16,32,1280]{2,1,0:T(8,128)(2,1)}, u32[]{:S(2)}, u32[]{:S(2)}) %all-to-all-start.2) | async-done | bytes 1310752 | tf_op jit(solution)/shard_map/all_to_all | solution.py:301
  142.0 4.6 %all-to-all-start.3 = ((bf16[16,32,1280]{2,1,0:T(8,128)(2,1)}), bf16[16,32,1280]{2,1,0:T(8,128)(2,1)}, u32[]{:S(2)}, u32[]{:S(2)}) async-start(bf16[16,32,1280]{2,1,0:T(8,128)(2,1)} %shard_map.88), calls=%async_computation.3 | async-start | bytes 2621440 | tf_op jit(solution)/shard_map/all_to_all | solution.py:301
  149.7 6.8 %shard_map.89 = (bf16[1187,1280]{1,0:T(8,128)(2,1)}, f32[8,128]{1,0:T(8,128)S(1)}) custom-call(s32[8]{0:T(128)S(1)} %stack.59._, bf16[1200,128]{1,0:T(8,128)(2,1)S(1)} %copy-done.15, bf16[1200,128]{1,0:T(8,128)(2,1)S(1)} %copy-done.19, bf16[1200,128]{1,0:T(8,128)(2,1)S(1)} %copy-done.17, bf16[1200,128]{1,0:T(8,128)(2,1)S(1)} %copy-done.21, ...), custom_call_target="tpu_custom_call" | custom-call | flops 3111649280 | bytes 6077440 | tf_op jit(solution)/shard_map/pallas_call | solution.py:337
  156.6 1.5 convert_reduce_fusion.1
  158.1 8.8 %all-to-all-done.3 = bf16[16,32,1280]{2,1,0:T(8,128)(2,1)} async-done(((bf16[16,32,1280]{2,1,0:T(8,128)(2,1)}), bf16[16,32,1280]{2,1,0:T(8,128)(2,1)}, u32[]{:S(2)}, u32[]{:S(2)}) %all-to-all-start.3) | async-done | bytes 1310752 | tf_op jit(solution)/shard_map/all_to_all | solution.py:301
  166.9 1.5 convert_reduce_fusion
  169.8 2.6 %collective-permute-start.21 = (f32[16,1280]{1,0:T(8,128)S(1)}, f32[16,1280]{1,0:T(8,128)S(1)}, u32[]{:S(2)}, u32[]{:S(2)}) collective-permute-start(f32[16,1280]{1,0:T(8,128)S(1)} %get-tuple-element.49), channel_id=1, source_target_pairs={{0,48},{16,0},{32,16},{48,32},{1,49},{17,1},{33,17},{49,33},{2,50}... | collective-permute-start | bytes 245768 | tf_op jit(solution)/shard_map/ppermute | solution.py:40
  (104 shorter events, 28.4 us)
Async XLA Ops:
  1.9 2.8 %copy-start = (bf16[1024,1280]{1,0:T(8,128)(2,1)S(1)}, bf16[1024,1280]{1,0:T(8,128)(2,1)}, u32[]{:S(2)}) copy-start(bf16[1024,1280]{1,0:T(8,128)(2,1)} %refs_15_.1) | copy-start | bytes 7864324
  1.9 3.4 %copy-start.4 = (bf16[1280,1187]{0,1:T(8,128)(2,1)S(1)}, bf16[1280,1187]{0,1:T(8,128)(2,1)}, u32[]{:S(2)}) copy-start(bf16[1280,1187]{0,1:T(8,128)(2,1)} %param.8) | copy-start | bytes 9116164
  4.6 4.3 %collective-permute-start.1 = (f32[1187,256]{1,0:T(8,128)S(1)}, f32[1187,256]{1,0:T(8,128)S(1)}, u32[]{:S(2)}, u32[]{:S(2)}) collective-permute-start(f32[1187,256]{1,0:T(8,128)S(1)} %convolution_bitcast_fusion.2), channel_id=1, source_target_pairs={{0,64},{64,0},{1,65},{65,1},{2,66},{66,2},{3,67},{67,3},{4,68},{68... | collective-permute-start | bytes 3646472 | tf_op jit(solution)/shard_map/ppermute | solution.py:36
  6.3 3.0 %collective-permute-start = (f32[1187,256]{1,0:T(8,128)S(1)}, f32[1187,256]{1,0:T(8,128)S(1)}, u32[]{:S(2)}, u32[]{:S(2)}) collective-permute-start(f32[1187,256]{1,0:T(8,128)S(1)} %convolution_bitcast_fusion), channel_id=1, source_target_pairs={{0,64},{64,0},{1,65},{65,1},{2,66},{66,2},{3,67},{67,3},{4,68},{68... | collective-permute-start | bytes 3646472 | tf_op jit(solution)/shard_map/ppermute | solution.py:36
  9.0 7.6 %copy-start.27 = (s32[256]{0:T(256)S(1)}, s32[256]{0:T(256)}, u32[]{:S(2)}) copy-start(s32[256]{0:T(256)} %param.9) | copy-start | bytes 3076
  11.0 23.5 %collective-permute-start.4 = (s16[2,1200,128]{2,1,0:T(8,128)(2,1)}, s16[2,1200,128]{2,1,0:T(8,128)(2,1)S(1)}, u32[]{:S(2)}, u32[]{:S(2)}) collective-permute-start(s16[2,1200,128]{2,1,0:T(8,128)(2,1)} %shard_map.76), channel_id=1, source_target_pairs={{0,128},{128,0},{1,129},{129,1},{2,130},{130,2},{3,131},{131,3},{4... | collective-permute-start | bytes 1843208 | tf_op jit(solution)/shard_map/ppermute | solution.py:36
  16.5 1.2 collective-permute-start.5
  16.7 88.1 %copy-start.26 = (s32[3]{0:T(128)}, s32[3]{0:T(128)S(1)}, u32[]{:S(2)}) copy-start(s32[3]{0:T(128)S(1)} %pad_add_fusion.place) | copy-start | bytes 40
  33.0 7.2 %collective-permute-start.2 = (f32[1187,256]{1,0:T(8,128)S(1)}, f32[1187,256]{1,0:T(8,128)S(1)}, u32[]{:S(2)}, u32[]{:S(2)}) collective-permute-start(f32[1187,256]{1,0:T(8,128)S(1)} %get-tuple-element.25), channel_id=1, source_target_pairs={{0,64},{64,0},{1,65},{65,1},{2,66},{66,2},{3,67},{67,3},{4,68},{68... | collective-permute-start | bytes 3646472 | tf_op jit(solution)/shard_map/ppermute | solution.py:36
  33.3 6.9 %collective-permute-start.3 = (f32[1187,256]{1,0:T(8,128)S(1)}, f32[1187,256]{1,0:T(8,128)S(1)}, u32[]{:S(2)}, u32[]{:S(2)}) collective-permute-start(f32[1187,256]{1,0:T(8,128)S(1)} %get-tuple-element.27), channel_id=1, source_target_pairs={{0,64},{64,0},{1,65},{65,1},{2,66},{66,2},{3,67},{67,3},{4,68},{68... | collective-permute-start | bytes 3646472 | tf_op jit(solution)/shard_map/ppermute | solution.py:36
  34.6 34.6 %collective-permute-start.11 = (s16[2,1200,128]{2,1,0:T(8,128)(2,1)S(1)}, s16[2,1200,128]{2,1,0:T(8,128)(2,1)S(1)}, u32[]{:S(2)}, u32[]{:S(2)}) collective-permute-start(s16[2,1200,128]{2,1,0:T(8,128)(2,1)S(1)} %shard_map.77), channel_id=1, source_target_pairs={{0,128},{128,0},{1,129},{129,1},{2,130},{130,2},{3,131},{131,3},{4... | collective-permute-start | bytes 1843208 | tf_op jit(solution)/shard_map/ppermute | solution.py:36
  65.2 9.5 %collective-permute-start.8 = (f32[8,128]{1,0:T(8,128)S(1)}, f32[8,128]{1,0:T(8,128)S(1)}, u32[]{:S(2)}, u32[]{:S(2)}) collective-permute-start(f32[8,128]{1,0:T(8,128)S(1)} %shard_map.81.s0), channel_id=1, source_target_pairs={{0,48},{16,0},{32,16},{48,32},{1,49},{17,1},{33,17},{49,33},{2,50}... | collective-permute-start | bytes 12296 | tf_op jit(solution)/shard_map/ppermute | solution.py:40
  65.3 10.8 %collective-permute-start.7 = (f32[8,128]{1,0:T(8,128)S(1)}, f32[8,128]{1,0:T(8,128)S(1)}, u32[]{:S(2)}, u32[]{:S(2)}) collective-permute-start(f32[8,128]{1,0:T(8,128)S(1)} %shard_map.81.s0), channel_id=1, source_target_pairs={{0,32},{16,48},{32,0},{48,16},{1,33},{17,49},{33,1},{49,17},{2,34}... | collective-permute-start | bytes 12296 | tf_op jit(solution)/shard_map/ppermute | solution.py:40
  68.3 7.9 %collective-permute-start.6 = (f32[8,128]{1,0:T(8,128)S(1)}, f32[8,128]{1,0:T(8,128)S(1)}, u32[]{:S(2)}, u32[]{:S(2)}) collective-permute-start(f32[8,128]{1,0:T(8,128)S(1)} %shard_map.81.s0), channel_id=1, source_target_pairs={{0,16},{16,32},{32,48},{48,0},{1,17},{17,33},{33,49},{49,1},{2,18}... | collective-permute-start | bytes 12296 | tf_op jit(solution)/shard_map/ppermute | solution.py:40
  77.4 22.1 %copy-start.14 = (bf16[1200,128]{1,0:T(8,128)(2,1)}, bf16[1200,128]{1,0:T(8,128)(2,1)S(1)}, u32[]{:S(2)}) copy-start(bf16[1200,128]{1,0:T(8,128)(2,1)S(1)} %shard_map.82.refs_0_) | copy-start | bytes 921604
  77.4 29.4 %collective-permute-start.10 = (bf16[1200,128]{1,0:T(8,128)(2,1)S(1)}, bf16[1200,128]{1,0:T(8,128)(2,1)S(1)}, u32[]{:S(2)}, u32[]{:S(2)}) collective-permute-start(bf16[1200,128]{1,0:T(8,128)(2,1)S(1)} %shard_map.82.refs_0_), channel_id=1, source_target_pairs={{0,128},{128,0},{1,129},{129,1},{2,130},{130,2},{3,131},{131,3},{4... | collective-permute-start | bytes 921608 | tf_op jit(solution)/shard_map/ppermute | solution.py:36
  97.3 3.7 %collective-permute-start.14 = (f32[8,128]{1,0:T(8,128)S(1)}, f32[8,128]{1,0:T(8,128)S(1)}, u32[]{:S(2)}, u32[]{:S(2)}) collective-permute-start(f32[8,128]{1,0:T(8,128)S(1)} %shard_map.85.s0), channel_id=1, source_target_pairs={{0,48},{16,0},{32,16},{48,32},{1,49},{17,1},{33,17},{49,33},{2,50}... | collective-permute-start | bytes 12296 | tf_op jit(solution)/shard_map/ppermute | solution.py:40
  97.4 4.6 %collective-permute-start.13 = (f32[8,128]{1,0:T(8,128)S(1)}, f32[8,128]{1,0:T(8,128)S(1)}, u32[]{:S(2)}, u32[]{:S(2)}) collective-permute-start(f32[8,128]{1,0:T(8,128)S(1)} %shard_map.85.s0), channel_id=1, source_target_pairs={{0,32},{16,48},{32,0},{48,16},{1,33},{17,49},{33,1},{49,17},{2,34}... | collective-permute-start | bytes 12296 | tf_op jit(solution)/shard_map/ppermute | solution.py:40
  99.4 5.4 %collective-permute-start.12 = (f32[8,128]{1,0:T(8,128)S(1)}, f32[8,128]{1,0:T(8,128)S(1)}, u32[]{:S(2)}, u32[]{:S(2)}) collective-permute-start(f32[8,128]{1,0:T(8,128)S(1)} %shard_map.85.s0), channel_id=1, source_target_pairs={{0,16},{16,32},{32,48},{48,0},{1,17},{17,33},{33,49},{49,1},{2,18}... | collective-permute-start | bytes 12296 | tf_op jit(solution)/shard_map/ppermute | solution.py:40
  99.4 9.4 %collective-permute-start.9 = (bf16[1200,128]{1,0:T(8,128)(2,1)S(1)}, bf16[1200,128]{1,0:T(8,128)(2,1)S(1)}, u32[]{:S(2)}, u32[]{:S(2)}) collective-permute-start(bf16[1200,128]{1,0:T(8,128)(2,1)S(1)} %shard_map.82.refs_0_), channel_id=1, source_target_pairs={{0,64},{64,0},{1,65},{65,1},{2,66},{66,2},{3,67},{67,3},{4,68},{68... | collective-permute-start | bytes 921608 | tf_op jit(solution)/shard_map/ppermute | solution.py:36
  106.7 2.1 %collective-permute-start.15 = (bf16[1200,128]{1,0:T(8,128)(2,1)S(1)}, bf16[1200,128]{1,0:T(8,128)(2,1)S(1)}, u32[]{:S(2)}, u32[]{:S(2)}) collective-permute-start(bf16[1200,128]{1,0:T(8,128)(2,1)S(1)} %collective-permute-done.10.refs_2_), channel_id=1, source_target_pairs={{0,64},{64,0},{1,65},{65,1},{2,66},{66,2},{3,67},{67,3},{4,68},{68... | collective-permute-start | bytes 921608 | tf_op jit(solution)/shard_map/ppermute | solution.py:36
  106.8 18.9 %collective-permute-start.17 = (bf16[1200,128]{1,0:T(8,128)(2,1)}, bf16[1200,128]{1,0:T(8,128)(2,1)}, u32[]{:S(2)}, u32[]{:S(2)}) collective-permute-start(bf16[1200,128]{1,0:T(8,128)(2,1)} %shard_map.86.refs_0_.refs_4_), channel_id=1, source_target_pairs={{0,128},{128,0},{1,129},{129,1},{2,130},{130,2},{3,131},{131,3},{4... | collective-permute-start | bytes 921608 | tf_op jit(solution)/shard_map/ppermute | solution.py:36
  115.3 26.7 %all-to-all-start.2 = ((bf16[16,32,1280]{2,1,0:T(8,128)(2,1)}), bf16[16,32,1280]{2,1,0:T(8,128)(2,1)}, u32[]{:S(2)}, u32[]{:S(2)}) async-start(bf16[16,32,1280]{2,1,0:T(8,128)(2,1)} %shard_map.87), calls=%async_computation.2 | async-start | bytes 2621440 | tf_op jit(solution)/shard_map/all_to_all | solution.py:301
  119.7 6.0 %collective-permute-start.16 = (bf16[1200,128]{1,0:T(8,128)(2,1)}, bf16[1200,128]{1,0:T(8,128)(2,1)S(1)}, u32[]{:S(2)}, u32[]{:S(2)}) collective-permute-start(bf16[1200,128]{1,0:T(8,128)(2,1)} %shard_map.86.refs_0_.refs_4_), channel_id=1, source_target_pairs={{0,64},{64,0},{1,65},{65,1},{2,66},{66,2},{3,67},{67,3},{4,68},{68... | collective-permute-start | bytes 921608 | tf_op jit(solution)/shard_map/ppermute | solution.py:36
  125.7 1.8 %collective-permute-start.18 = (bf16[1200,128]{1,0:T(8,128)(2,1)}, bf16[1200,128]{1,0:T(8,128)(2,1)S(1)}, u32[]{:S(2)}, u32[]{:S(2)}) collective-permute-start(bf16[1200,128]{1,0:T(8,128)(2,1)} %collective-permute-done.17.refs_2_.refs_6_), channel_id=1, source_target_pairs={{0,64},{64,0},{1,65},{65,1},{2,66},{66,2},{3,67},{67,3},{4,68},{68... | collective-permute-start | bytes 921608 | tf_op jit(solution)/shard_map/ppermute | solution.py:36
  133.3 13.5 %copy-start.15 = (bf16[1200,128]{1,0:T(8,128)(2,1)S(1)}, bf16[1200,128]{1,0:T(8,128)(2,1)}, u32[]{:S(2)}) copy-start(bf16[1200,128]{1,0:T(8,128)(2,1)} %copy-done.14) | copy-start | bytes 921604
  133.3 13.5 %copy-start.17 = (bf16[1200,128]{1,0:T(8,128)(2,1)S(1)}, bf16[1200,128]{1,0:T(8,128)(2,1)}, u32[]{:S(2)}) copy-start(bf16[1200,128]{1,0:T(8,128)(2,1)} %copy-done.16) | copy-start | bytes 921604
  133.3 13.5 %copy-start.19 = (bf16[1200,128]{1,0:T(8,128)(2,1)S(1)}, bf16[1200,128]{1,0:T(8,128)(2,1)}, u32[]{:S(2)}) copy-start(bf16[1200,128]{1,0:T(8,128)(2,1)} %copy-done.18) | copy-start | bytes 921604
  142.0 24.9 %all-to-all-start.3 = ((bf16[16,32,1280]{2,1,0:T(8,128)(2,1)}), bf16[16,32,1280]{2,1,0:T(8,128)(2,1)}, u32[]{:S(2)}, u32[]{:S(2)}) async-start(bf16[16,32,1280]{2,1,0:T(8,128)(2,1)} %shard_map.88), calls=%async_computation.3 | async-start | bytes 2621440 | tf_op jit(solution)/shard_map/all_to_all | solution.py:301
  168.5 6.4 %collective-permute-start.19 = (f32[16,1280]{1,0:T(8,128)S(1)}, f32[16,1280]{1,0:T(8,128)S(1)}, u32[]{:S(2)}, u32[]{:S(2)}) collective-permute-start(f32[16,1280]{1,0:T(8,128)S(1)} %get-tuple-element.47), channel_id=1, source_target_pairs={{0,16},{16,32},{32,48},{48,0},{1,17},{17,33},{33,49},{49,1},{2,18}... | collective-permute-start | bytes 245768 | tf_op jit(solution)/shard_map/ppermute | solution.py:40
  168.6 6.3 %collective-permute-start.20 = (f32[16,1280]{1,0:T(8,128)S(1)}, f32[16,1280]{1,0:T(8,128)S(1)}, u32[]{:S(2)}, u32[]{:S(2)}) collective-permute-start(f32[16,1280]{1,0:T(8,128)S(1)} %get-tuple-element.48), channel_id=1, source_target_pairs={{0,32},{16,48},{32,0},{48,16},{1,33},{17,49},{33,1},{49,17},{2,34}... | collective-permute-start | bytes 245768 | tf_op jit(solution)/shard_map/ppermute | solution.py:40
  169.8 6.0 %collective-permute-start.21 = (f32[16,1280]{1,0:T(8,128)S(1)}, f32[16,1280]{1,0:T(8,128)S(1)}, u32[]{:S(2)}, u32[]{:S(2)}) collective-permute-start(f32[16,1280]{1,0:T(8,128)S(1)} %get-tuple-element.49), channel_id=1, source_target_pairs={{0,48},{16,0},{32,16},{48,32},{1,49},{17,1},{33,17},{49,33},{2,50}... | collective-permute-start | bytes 245768 | tf_op jit(solution)/shard_map/ppermute | solution.py:40
  (20 other events, 28.7 us)
